TPU v7x, 32 devices: a whole 2x2x4 slice. The times are simulated.
32 devices in a mesh: dp: 16 (over z, x, core), tensor: 2 (over y).
Axes of the slice: x: 2, y: 2, z: 4, core: 2. Of those that a mesh axis runs over, the one named last changes fastest.
Arguments:
- hidden_in: bfloat16 [4096, 1536], P(('dp', 'tensor')), may hold values from -6 to 6
- out_grad: bfloat16 [4096, 1536], P(('dp', 'tensor')), may hold values from -6 to 6
- routes_first: int32 [4096, 6], P('dp'), may hold values from 0 to 15, all different within a row; in each aligned block of 256 rows (0 to 255, 256 to 511, ...) at most 128 rows name the same one
- routes_second: int32 [4096, 6], P('dp'), may hold values from 0 to 15, all different within a row; in each aligned block of 256 rows (0 to 255, 256 to 511, ...) at most 128 rows name the same one
- in_gate: bfloat16 [1536, 3072], P('dp', 'tensor'), may hold values from -0.15625 to 0.15625
- in_value: bfloat16 [1536, 3072], P('dp', 'tensor'), may hold values from -0.15625 to 0.15625
- in_state: bfloat16 [1536, 256], P('dp', 'tensor'), may hold values from -0.15625 to 0.15625
- in_step: bfloat16 [1536, 48], P('dp', 'tensor'), may hold values from -0.15625 to 0.15625
- mix_output: bfloat16 [3072, 1536], P('tensor', 'dp'), may hold values from -0.109375 to 0.109375
- attn_query: bfloat16 [1536, 1536], P('dp', 'tensor'), may hold values from -0.15625 to 0.15625
- attention_key_matrix: bfloat16 [1536, 512], P('dp', 'tensor'), may hold values from -0.15625 to 0.15625
- attention_value_matrix: bfloat16 [1536, 512], P('dp', 'tensor'), may hold values from -0.15625 to 0.15625
- attn_output: bfloat16 [1536, 1536], P('tensor', 'dp'), may hold values from -1.25 to 1.25
- shared_gate_one: bfloat16 [1536, 1024], P('dp', 'tensor'), may hold values from -0.15625 to 0.15625
- shared_up_one: bfloat16 [1536, 1024], P('dp', 'tensor'), may hold values from -0.15625 to 0.15625
- shared_down_one: bfloat16 [1024, 1536], P('tensor', 'dp'), may hold values from -0.375 to 0.375
- shared_gate_two: bfloat16 [1536, 1024], P('dp', 'tensor'), may hold values from -0.15625 to 0.15625
- shared_up_two: bfloat16 [1536, 1024], P('dp', 'tensor'), may hold values from -0.15625 to 0.15625
- shared_down_two: bfloat16 [1024, 1536], P('tensor', 'dp'), may hold values from -0.375 to 0.375
- expert_gate_one: bfloat16 [16, 1536, 512], P('dp', None, 'tensor'), may hold values from -0.15625 to 0.15625
- expert_up_one: bfloat16 [16, 1536, 512], P('dp', None, 'tensor'), may hold values from -0.15625 to 0.15625
- expert_down_one: bfloat16 [16, 512, 1536], P('dp', 'tensor'), may hold values from -0.5 to 0.5
- expert_gate_two: bfloat16 [16, 1536, 512], P('dp', None, 'tensor'), may hold values from -0.15625 to 0.15625
- expert_up_two: bfloat16 [16, 1536, 512], P('dp', None, 'tensor'), may hold values from -0.15625 to 0.15625
- expert_down_two: bfloat16 [16, 512, 1536], P('dp', 'tensor'), may hold values from -0.5 to 0.5
- router_one: bfloat16 [1536, 16], replicated, may hold values from -0.078125 to 0.078125
- router_two: bfloat16 [1536, 16], replicated, may hold values from -0.078125 to 0.078125
- norm_mix: float32 [1536], replicated, may hold values from 0.5 to 1.5
- norm_moe_one: float32 [1536], replicated, may hold values from 0.5 to 1.5
- norm_attn: float32 [1536], replicated, may hold values from 0.5 to 1.5
- norm_moe_two: float32 [1536], replicated, may hold values from 0.5 to 1.5
- gated_norm: float32 [3072], replicated, may hold values from 0.5 to 1.5
- conv_value_weight: float32 [4, 3072], replicated, may hold values from -3 to 3
- conv_value_bias: float32 [3072], replicated, may hold values from -0.5 to 0.5
- conv_state_weight: float32 [4, 256], replicated, may hold values from -3 to 3
- conv_state_bias: float32 [256], replicated, may hold values from -0.5 to 0.5
- step_bias: float32 [48], replicated, may hold values from -6 to -2
- decay_log: float32 [48], replicated, may hold values from 0 to 1.5
- skip_gain: float32 [48], replicated, may hold values from 0.5 to 1.5
Outputs:
- block_out: float32 [4096, 1536], P(('dp', 'tensor'))
- input_grad: float32 [4096, 1536], P(('dp', 'tensor'))
- grad_in_gate: float32 [1536, 3072], P('dp', 'tensor')
- grad_in_value: float32 [1536, 3072], P('dp', 'tensor')
- grad_in_state: float32 [1536, 256], P('dp', 'tensor')
- grad_in_step: float32 [1536, 48], P('dp', 'tensor')
- grad_mix_output: float32 [3072, 1536], P('tensor', 'dp')
- grad_attn_query: float32 [1536, 1536], P('dp', 'tensor')
- grad_attn_key: float32 [1536, 512], P('dp', 'tensor')
- grad_attn_value: float32 [1536, 512], P('dp', 'tensor')
- grad_attn_output: float32 [1536, 1536], P('tensor', 'dp')
- grad_shared_gate_one: float32 [1536, 1024], P('dp', 'tensor')
- grad_shared_up_one: float32 [1536, 1024], P('dp', 'tensor')
- grad_shared_down_one: float32 [1024, 1536], P('tensor', 'dp')
- grad_shared_gate_two: float32 [1536, 1024], P('dp', 'tensor')
- grad_shared_up_two: float32 [1536, 1024], P('dp', 'tensor')
- grad_shared_down_two: float32 [1024, 1536], P('tensor', 'dp')
- grad_expert_gate_one: float32 [16, 1536, 512], P('dp', None, 'tensor')
- grad_expert_up_one: float32 [16, 1536, 512], P('dp', None, 'tensor')
- grad_expert_down_one: float32 [16, 512, 1536], P('dp', 'tensor')
- grad_expert_gate_two: float32 [16, 1536, 512], P('dp', None, 'tensor')
- grad_expert_up_two: float32 [16, 1536, 512], P('dp', None, 'tensor')
- grad_expert_down_two: float32 [16, 512, 1536], P('dp', 'tensor')
- grad_router_one: float32 [1536, 16], replicated
- grad_router_two: float32 [1536, 16], replicated
- grad_norm_mix: float32 [1536], replicated
- grad_norm_moe_one: float32 [1536], replicated
- grad_norm_attn: float32 [1536], replicated
- grad_norm_moe_two: float32 [1536], replicated
- grad_gated_norm: float32 [3072], replicated
- grad_conv_value_weight: float32 [4, 3072], replicated
- grad_conv_value_bias: float32 [3072], replicated
- grad_conv_state_weight: float32 [4, 256], replicated
- grad_conv_state_bias: float32 [256], replicated
- grad_step_bias: float32 [48], replicated
- grad_decay_log: float32 [48], replicated
- grad_skip_gain: float32 [48], replicated
Inputs may be any that keep to these rules, and one draw needn't show every extreme that they name: `routes_first`: each row names 6 different experts. In the 256 rows of one sequence no expert is named more than 128 times, and in some sequence one expert is named exactly 128 times. `routes_second`: as for routes_first.
All inputs are finite; a program needn't handle non-finite values.
Results may differ from a plain program's by a relative error of at most 0.039.
Values may be sent and summed in bfloat16 or wider, within the bound.
No kernel may reach another device: no remote copies, remote signals or barrier semaphores. Data moves between devices by JAX's collectives and lax.ppermute only.
A program may use at most 384 MiB of HBM per device.

v0:
```python
import jax
import jax.numpy as jnp
from jax import lax
from jax.sharding import PartitionSpec as P

MH = 48
NS = 128
CH = 128
QUERY_HEADS = 12
KEY_VALUE_HEADS = 4
HEAD_SIZE = 128
TOP = 6
LEN = 256
DI = 3072


EPS = 1e-05
HIGH = lax.Precision.HIGHEST


def matmul(left, right):
    return jnp.dot(left, right, preferred_element_type=jnp.float32)


def times_back(left, right):
    return lax.dot_general(
        left, right, (((1,), (1,)), ((), ())), preferred_element_type=jnp.float32
    )


def times_over(left, right):
    return lax.dot_general(
        left, right, (((0,), (0,)), ((), ())), preferred_element_type=jnp.float32
    )


def rms_norm(value_rows, gain):
    return value_rows * lax.rsqrt(jnp.mean(value_rows * value_rows, -1, keepdims=True) + EPS) * gain


def causal_conv(value_rows, weight, bias):
    width = weight.shape[0]
    sequence_length = value_rows.shape[0]
    padded = jnp.concatenate(
        [jnp.zeros((width - 1, value_rows.shape[1]), jnp.float32), value_rows], 0
    )
    total = jnp.zeros_like(value_rows) + bias[None, :]
    for shift in range(width):
        total = total + weight[shift][None, :] * padded[shift : shift + sequence_length]
    return total


def conv_act(value_rows, weight, bias):
    return jax.nn.silu(causal_conv(value_rows, weight, bias))


def state_scan(heads_in, delta, rate, in_map, out_map):
    sequence_length, heads, width = heads_in.shape
    count = sequence_length // CH
    blocks = (
        heads_in.reshape(count, CH, heads, width),
        delta.reshape(count, CH, heads),
        in_map.reshape(count, CH, -1),
        out_map.reshape(count, CH, -1),
    )
    lower = (jnp.arange(CH)[:, None] >= jnp.arange(CH)[None, :])[:, :, None]

    def advance(state, block):
        x_blk, d_blk, b_blk, c_blk = block
        cum = jnp.cumsum(d_blk * rate[None, :], 0)
        diff = jnp.where(lower, cum[:, None, :] - cum[None, :, :], 0.0)
        decay = jnp.where(lower, jnp.exp(diff), 0.0)
        inner = jnp.dot(c_blk, b_blk.T, precision=HIGH)
        weights = inner[:, :, None] * decay * d_blk[None, :, :]
        local = jnp.einsum("ijh,jhp->ihp", weights, x_blk, precision=HIGH)
        carried = jnp.exp(cum)[:, :, None] * jnp.einsum("in,hpn->ihp", c_blk, state, precision=HIGH)
        tail = jnp.exp(cum[-1][None, :] - cum) * d_blk
        update = jnp.einsum("jhp,jn->hpn", tail[:, :, None] * x_blk, b_blk, precision=HIGH)
        return (jnp.exp(cum[-1])[:, None, None] * state + update, local + carried)

    start = jnp.zeros((heads, width, in_map.shape[1]), jnp.float32)
    _, outs = lax.scan(advance, start, blocks)
    return outs.reshape(sequence_length, heads, width)


def scan_part(value_act, step_pre, step_bias, decay_log, skip_gain, in_map, out_map):
    sequence_length = value_act.shape[0]
    heads = step_pre.shape[1]
    heads_in = value_act.reshape(sequence_length, heads, -1)
    delta = jax.nn.softplus(step_pre + step_bias[None, :])
    rate = -jnp.exp(decay_log)
    outs = state_scan(heads_in, delta, rate, in_map, out_map) + skip_gain[None, :, None] * heads_in
    return outs.reshape(sequence_length, -1)


def expert_plan(routes, count, cap):
    flat = routes.reshape(-1)
    table = (flat[:, None] == jnp.arange(count, dtype=jnp.int32)[None, :]).astype(jnp.int32)
    before = jnp.sum((jnp.cumsum(table, 0) - table) * table, 1)
    slot = flat * cap + before
    order = jnp.arange(flat.shape[0], dtype=jnp.int32)
    source = jnp.zeros((count * cap,), jnp.int32).at[slot].set(order)
    filled = jnp.zeros((count * cap,), jnp.int32).at[slot].set(1)
    return (slot, source, filled > 0)


def silu_slope(value_rows):
    sig = jax.nn.sigmoid(value_rows)
    return sig * (1.0 + value_rows * (1.0 - sig))


def widen(value_rows, start, total, axis):
    shape = list(value_rows.shape)
    shape[axis] = total
    return lax.dynamic_update_slice_in_dim(jnp.zeros(shape, jnp.float32), value_rows, start, axis)


def routed_expert_forward(token_portion, expert_gate_weight, expert_up_weight, expert_down_weight):
    first = jnp.einsum(
        "vaq,qr->var", token_portion, expert_gate_weight, preferred_element_type=jnp.float32
    )
    latter_half = jnp.einsum(
        "vaq,qr->var", token_portion, expert_up_weight, preferred_element_type=jnp.float32
    )
    hidden = (jax.nn.silu(first) * latter_half).astype(jnp.bfloat16)
    return jnp.einsum("scf,fd->scd", hidden, expert_down_weight, preferred_element_type=jnp.float32)


def routed_expert_backward(
    token_portion, gradient_output, expert_gate_weight, expert_up_weight, expert_down_weight
):
    first = jnp.einsum(
        "vaq,qr->var", token_portion, expert_gate_weight, preferred_element_type=jnp.float32
    )
    latter_half = jnp.einsum(
        "vaq,qr->var", token_portion, expert_up_weight, preferred_element_type=jnp.float32
    )
    active = jax.nn.silu(first)
    hidden = (active * latter_half).astype(jnp.bfloat16)
    d_hidden = jnp.einsum(
        "scd,fd->scf", gradient_output, expert_down_weight, preferred_element_type=jnp.float32
    )
    d_first = (d_hidden * latter_half * silu_slope(first)).astype(jnp.bfloat16)
    gradient_latter = (d_hidden * active).astype(jnp.bfloat16)
    d_piece = jnp.einsum(
        "vxm,rm->vxr", d_first, expert_gate_weight, preferred_element_type=jnp.float32
    ) + jnp.einsum(
        "vxm,rm->vxr", gradient_latter, expert_up_weight, preferred_element_type=jnp.float32
    )
    return (d_piece, d_first, gradient_latter, hidden)


def weight_grads(token_portion, gradient_output, d_first, gradient_latter, hidden):
    expert_gate_gradient = jnp.einsum(
        "awl,awv->lv", token_portion, d_first, preferred_element_type=jnp.float32
    )[None]
    expert_up_gradient = jnp.einsum(
        "awl,awv->lv", token_portion, gradient_latter, preferred_element_type=jnp.float32
    )[None]
    expert_down_gradient = jnp.einsum(
        "scf,scd->fd", hidden, gradient_output, preferred_element_type=jnp.float32
    )[None]
    return (expert_gate_gradient, expert_up_gradient, expert_down_gradient)


def body(
    hidden_in,
    out_grad,
    routes_first,
    routes_second,
    in_gate,
    in_value,
    in_state,
    in_step,
    mix_output,
    attn_query,
    attention_key_matrix,
    attention_value_matrix,
    attn_output,
    shared_gate_one,
    shared_up_one,
    shared_down_one,
    shared_gate_two,
    shared_up_two,
    shared_down_two,
    expert_gate_one,
    expert_up_one,
    expert_down_one,
    expert_gate_two,
    expert_up_two,
    expert_down_two,
    router_one,
    router_two,
    norm_mix,
    norm_moe_one,
    norm_attn,
    norm_moe_two,
    gated_norm,
    conv_value_weight,
    conv_value_bias,
    conv_state_weight,
    conv_state_bias,
    step_bias,
    decay_log,
    skip_gain,
):
    tensor_rank = lax.axis_index("tensor")
    expert_count = lax.axis_size("dp")
    capacity = LEN * TOP * 4 // (3 * expert_count)
    local_rows = hidden_in.shape[0]
    row_start = tensor_rank * local_rows
    value_cols = in_value.shape[1]
    state_cols = in_state.shape[1]
    head_cols = in_step.shape[1]
    value_start = tensor_rank * value_cols
    state_start = tensor_rank * state_cols
    head_start = tensor_rank * head_cols
    norm_local = lax.dynamic_slice_in_dim(gated_norm, value_start, value_cols, 0)
    value_kernel = lax.dynamic_slice_in_dim(conv_value_weight, value_start, value_cols, 1)
    value_offset = lax.dynamic_slice_in_dim(conv_value_bias, value_start, value_cols, 0)
    state_kernel = lax.dynamic_slice_in_dim(conv_state_weight, state_start, state_cols, 1)
    state_offset = lax.dynamic_slice_in_dim(conv_state_bias, state_start, state_cols, 0)
    bias_local = lax.dynamic_slice_in_dim(step_bias, head_start, head_cols, 0)
    decay_local = lax.dynamic_slice_in_dim(decay_log, head_start, head_cols, 0)
    skip_local = lax.dynamic_slice_in_dim(skip_gain, head_start, head_cols, 0)
    scale = HEAD_SIZE ** (-0.5)

    def gather_mixer():
        return (
            lax.all_gather(in_gate, "dp", axis=0, tiled=True),
            lax.all_gather(in_value, "dp", axis=0, tiled=True),
            lax.all_gather(in_state, "dp", axis=0, tiled=True),
            lax.all_gather(in_step, "dp", axis=0, tiled=True),
            lax.all_gather(mix_output, "dp", axis=1, tiled=True),
            lax.all_gather(shared_gate_one, "dp", axis=0, tiled=True),
            lax.all_gather(shared_up_one, "dp", axis=0, tiled=True),
            lax.all_gather(shared_down_one, "dp", axis=1, tiled=True),
        )

    def gather_attention():
        return (
            lax.all_gather(attn_query, "dp", axis=0, tiled=True),
            lax.all_gather(attention_key_matrix, "dp", axis=0, tiled=True),
            lax.all_gather(attention_value_matrix, "dp", axis=0, tiled=True),
            lax.all_gather(attn_output, "dp", axis=1, tiled=True),
            lax.all_gather(shared_gate_two, "dp", axis=0, tiled=True),
            lax.all_gather(shared_up_two, "dp", axis=0, tiled=True),
            lax.all_gather(shared_down_two, "dp", axis=1, tiled=True),
        )

    def rows_in(value_rows):
        return lax.all_gather(value_rows, "tensor", axis=0, tiled=True)

    def rows_out(value_rows):
        return lax.psum_scatter(
            value_rows.astype(jnp.bfloat16), "tensor", scatter_dimension=0, tiled=True
        ).astype(jnp.float32)

    def norm_total(value_rows):
        return lax.psum(value_rows, "tensor")

    def send_back(value_rows):
        return lax.all_to_all(
            value_rows.astype(jnp.bfloat16), "dp", split_axis=0, concat_axis=0, tiled=True
        ).astype(value_rows.dtype)

    def route_rows(value_rows, slot, sequence_length):
        flat = value_rows.reshape(-1, value_rows.shape[-1])
        chosen_rows = flat[slot]
        return chosen_rows.reshape(sequence_length, TOP, -1)

    def moe_forward(rows, gain, router, routes, shared, expert_bank):
        w_sgate, w_sup, w_sdown = shared
        expert_gate_weight = expert_bank[0][0]
        expert_up_weight = expert_bank[1][0]
        expert_down_weight = expert_bank[2][0]
        normalized_input, norm_pull = jax.vjp(rms_norm, rows, gain)
        full = rows_in(normalized_input.astype(jnp.bfloat16))
        sequence_length = full.shape[0]
        logits = matmul(full, router)
        picked = routes[:, :, None] == jnp.arange(expert_count, dtype=jnp.int32)[None, None, :]
        gates = jax.nn.softmax(jnp.sum(jnp.where(picked, logits[:, None, :], 0.0), 2), 1)
        slot, source, filled = expert_plan(routes, expert_count, capacity)
        taken = jnp.where(filled[:, None], full[source // TOP], jnp.zeros((), jnp.bfloat16))
        taken = taken.reshape(expert_count, capacity, -1)
        results = send_back(
            routed_expert_forward(
                lax.all_to_all(taken, "dp", split_axis=0, concat_axis=0, tiled=True),
                expert_gate_weight,
                expert_up_weight,
                expert_down_weight,
            )
        )
        routed = route_rows(results, slot, sequence_length)
        shared_a = matmul(full, w_sgate)
        shared_b = matmul(full, w_sup)
        shared_h = (jax.nn.silu(shared_a) * shared_b).astype(jnp.bfloat16)
        partial_sum = matmul(shared_h, w_sdown) + jnp.sum(gates[:, :, None] * routed, 1)
        keep = (
            norm_pull,
            full,
            gates,
            picked,
            slot,
            source,
            filled,
            taken,
            routed,
            shared_a,
            shared_b,
            shared_h,
        )
        return (rows + rows_out(partial_sum), keep)

    def moe_backward(grad, router, shared, expert_bank, keep):
        w_sgate, w_sup, w_sdown = shared
        expert_gate_weight = expert_bank[0][0]
        expert_up_weight = expert_bank[1][0]
        expert_down_weight = expert_bank[2][0]
        (
            norm_pull,
            full,
            gates,
            picked,
            slot,
            source,
            filled,
            taken,
            routed,
            shared_a,
            shared_b,
            shared_h,
        ) = keep
        sequence_length = full.shape[0]
        dfull = rows_in(grad.astype(jnp.bfloat16))
        dwide = dfull.astype(jnp.float32)
        d_gates = jnp.sum(dwide[:, None, :] * routed, 2)
        d_routed = (
            (gates[:, :, None] * dwide[:, None, :])
            .astype(jnp.bfloat16)
            .reshape(sequence_length * TOP, -1)
        )
        d_taken = jnp.where(filled[:, None], d_routed[source], jnp.zeros((), jnp.bfloat16))
        d_taken = d_taken.reshape(expert_count, capacity, -1)
        dispatched_rows = lax.all_to_all(taken, "dp", split_axis=0, concat_axis=0, tiled=True)
        gradient_dispatched = lax.all_to_all(d_taken, "dp", split_axis=0, concat_axis=0, tiled=True)
        gradient_portion, gradient_first_layer, gradient_second_layer, expert_hidden = (
            routed_expert_backward(
                dispatched_rows,
                gradient_dispatched,
                expert_gate_weight,
                expert_up_weight,
                expert_down_weight,
            )
        )
        back = send_back(gradient_portion)
        g_experts = weight_grads(
            dispatched_rows,
            gradient_dispatched,
            gradient_first_layer,
            gradient_second_layer,
            expert_hidden,
        )
        d_experts = jnp.sum(route_rows(back, slot, sequence_length), 1)
        d_shared = times_back(dfull, w_sdown)
        low_sa = (d_shared * shared_b * silu_slope(shared_a)).astype(jnp.bfloat16)
        low_sb = (d_shared * jax.nn.silu(shared_a)).astype(jnp.bfloat16)
        d_normed = times_back(low_sa, w_sgate) + times_back(low_sb, w_sup) + d_experts
        g_shared = (times_over(full, low_sa), times_over(full, low_sb), times_over(shared_h, dfull))
        d_local, dg_local = (
            lax.psum_scatter(
                d_normed.astype(jnp.bfloat16), "tensor", scatter_dimension=0, tiled=True
            ).astype(jnp.float32),
            lax.psum_scatter(
                d_gates.astype(jnp.bfloat16), "tensor", scatter_dimension=0, tiled=True
            ).astype(jnp.float32),
        )
        gates_local = lax.dynamic_slice_in_dim(gates, row_start, local_rows, 0)
        picked_local = lax.dynamic_slice_in_dim(picked, row_start, local_rows, 0)
        d_chosen = gates_local * (dg_local - jnp.sum(gates_local * dg_local, 1, keepdims=True))
        d_logits = jnp.sum(jnp.where(picked_local, d_chosen[:, :, None], 0.0), 1).astype(
            jnp.bfloat16
        )
        d_local = d_local + times_back(d_logits, router)
        g_router = times_over(lax.dynamic_slice_in_dim(full, row_start, local_rows, 0), d_logits)
        d_rows, g_gain = norm_pull(d_local)
        return (grad + d_rows, g_gain, g_router, g_shared, g_experts)

    def attention_backward(grad, weights, keep):
        query_weight, key_weight, value_weight, w_out = weights
        norm_pull, full, query_rows, key_rows, value_rows, attended, logsum = keep
        sequence_length = full.shape[0]
        dfull = rows_in(grad.astype(jnp.bfloat16))
        d_att = times_back(dfull, w_out).astype(jnp.bfloat16).reshape(query_rows.shape)
        g_out = times_over(attended, dfull)
        causal = jnp.arange(sequence_length)[:, None] >= jnp.arange(sequence_length)[None, :]
        scores = (
            jnp.einsum("ikgd,jkd->kgij", query_rows, key_rows, preferred_element_type=jnp.float32)
            * scale
        )
        scores = jnp.where(causal, scores, -1e30)
        probs = jnp.exp(scores - logsum)
        d_probs = jnp.einsum(
            "ikgd,jkd->kgij", d_att, value_rows, preferred_element_type=jnp.float32
        )
        d_scores = (probs * (d_probs - jnp.sum(probs * d_probs, 3, keepdims=True))).astype(
            jnp.bfloat16
        )
        d_query = (
            (
                jnp.einsum("kgij,jkd->ikgd", d_scores, key_rows, preferred_element_type=jnp.float32)
                * scale
            )
            .astype(jnp.bfloat16)
            .reshape(sequence_length, -1)
        )
        d_keys = (
            (
                jnp.einsum(
                    "kgij,ikgd->jkd", d_scores, query_rows, preferred_element_type=jnp.float32
                )
                * scale
            )
            .astype(jnp.bfloat16)
            .reshape(sequence_length, -1)
        )
        d_values = (
            jnp.einsum(
                "kgij,ikgd->jkd",
                probs.astype(jnp.bfloat16),
                d_att,
                preferred_element_type=jnp.float32,
            )
            .astype(jnp.bfloat16)
            .reshape(sequence_length, -1)
        )
        d_normed = (
            times_back(d_query, query_weight)
            + times_back(d_keys, key_weight)
            + times_back(d_values, value_weight)
        )
        grads = (
            times_over(full, d_query),
            times_over(full, d_keys),
            times_over(full, d_values),
            g_out,
        )
        d_rows, g_gain = norm_pull(rows_out(d_normed))
        return (grad + d_rows, grads, g_gain)

    experts_one = (expert_gate_one, expert_up_one, expert_down_one)
    experts_two = (expert_gate_two, expert_up_two, expert_down_two)
    mixer_w = gather_mixer()
    rows = hidden_in.astype(jnp.float32)
    w_gate, value_weight, w_state, w_step, w_out = mixer_w[:5]
    normalized_input, norm_pull = jax.vjp(rms_norm, rows, norm_mix)
    full = rows_in(normalized_input.astype(jnp.bfloat16))
    gate_pre = matmul(full, w_gate)
    value_pre = matmul(full, value_weight)
    state_pre = matmul(full, w_state)
    step_pre = matmul(full, w_step)
    value_act, value_pull = jax.vjp(conv_act, value_pre, value_kernel, value_offset)
    state_act, state_pull = jax.vjp(conv_act, state_pre, state_kernel, state_offset)
    state_all = lax.all_gather(state_act.astype(jnp.bfloat16), "tensor", axis=1, tiled=True).astype(
        jnp.float32
    )
    ssm_out, scan_pull = jax.vjp(
        scan_part,
        value_act,
        step_pre,
        bias_local,
        decay_local,
        skip_local,
        state_all[:, :NS],
        state_all[:, NS:],
    )
    gated = ssm_out * jax.nn.silu(gate_pre)
    inverse = lax.rsqrt(norm_total(jnp.sum(gated * gated, 1)) / DI + EPS)[:, None]
    mixed = (gated * inverse * norm_local).astype(jnp.bfloat16)
    result = rows + rows_out(matmul(mixed, w_out))
    state_two, moe_one_keep = moe_forward(
        result, norm_moe_one, router_one, routes_first, mixer_w[5:], experts_one
    )
    attention_w = gather_attention()
    query_weight, key_weight, value_weight, w_out = attention_w[:4]
    normalized_input, attention_norm_pull = jax.vjp(rms_norm, state_two, norm_attn)
    attention_full = rows_in(normalized_input.astype(jnp.bfloat16))
    sequence_length = attention_full.shape[0]
    kv_heads = key_weight.shape[1] // HEAD_SIZE
    query_groups = QUERY_HEADS // KEY_VALUE_HEADS
    query_rows = (
        matmul(attention_full, query_weight)
        .astype(jnp.bfloat16)
        .reshape(sequence_length, kv_heads, query_groups, HEAD_SIZE)
    )
    key_rows = (
        matmul(attention_full, key_weight)
        .astype(jnp.bfloat16)
        .reshape(sequence_length, kv_heads, HEAD_SIZE)
    )
    value_rows = (
        matmul(attention_full, value_weight)
        .astype(jnp.bfloat16)
        .reshape(sequence_length, kv_heads, HEAD_SIZE)
    )
    causal = jnp.arange(sequence_length)[:, None] >= jnp.arange(sequence_length)[None, :]
    scores = (
        jnp.einsum("ikgd,jkd->kgij", query_rows, key_rows, preferred_element_type=jnp.float32)
        * scale
    )
    scores = jnp.where(causal, scores, -1e30)
    peak = jnp.max(scores, 3, keepdims=True)
    raised = jnp.exp(scores - peak)
    total = jnp.sum(raised, 3, keepdims=True)
    probs = (raised / total).astype(jnp.bfloat16)
    attended = jnp.einsum("kgij,jkd->ikgd", probs, value_rows, preferred_element_type=jnp.float32)
    attended = attended.reshape(sequence_length, -1).astype(jnp.bfloat16)
    result = state_two + rows_out(matmul(attended, w_out))
    attention_keep = (
        attention_norm_pull,
        attention_full,
        query_rows,
        key_rows,
        value_rows,
        attended,
        peak + jnp.log(total),
    )
    block_out, moe_two_keep = moe_forward(
        result, norm_moe_two, router_two, routes_second, attention_w[4:], experts_two
    )
    attention_b = gather_attention()
    grad = out_grad.astype(jnp.float32)
    grad, g_nmoe_two, g_router_two, g_shared_two, g_experts_two = moe_backward(
        grad, router_two, attention_b[4:], experts_two, moe_two_keep
    )
    grad, g_attention, g_nattn = attention_backward(grad, attention_b[:4], attention_keep)
    attention_sums = (
        lax.psum_scatter(g_attention[0], "dp", scatter_dimension=0, tiled=True),
        lax.psum_scatter(g_attention[1], "dp", scatter_dimension=0, tiled=True),
        lax.psum_scatter(g_attention[2], "dp", scatter_dimension=0, tiled=True),
        lax.psum_scatter(g_attention[3], "dp", scatter_dimension=1, tiled=True),
        lax.psum_scatter(g_shared_two[0], "dp", scatter_dimension=0, tiled=True),
        lax.psum_scatter(g_shared_two[1], "dp", scatter_dimension=0, tiled=True),
        lax.psum_scatter(g_shared_two[2], "dp", scatter_dimension=1, tiled=True),
    )
    mixer_b = gather_mixer()
    grad, g_nmoe_one, g_router_one, g_shared_one, g_experts_one = moe_backward(
        grad, router_one, mixer_b[5:], experts_one, moe_one_keep
    )
    w_gate, value_weight, w_state, w_step, w_out = mixer_b[:5]
    norm_pull, full, gate_pre, value_pull, state_pull, scan_pull, ssm_out, gated, inverse, mixed = (
        norm_pull,
        full,
        gate_pre,
        value_pull,
        state_pull,
        scan_pull,
        ssm_out,
        gated,
        inverse,
        mixed,
    )
    dfull = rows_in(grad.astype(jnp.bfloat16))
    d_mixed = times_back(dfull, w_out)
    g_out = times_over(mixed, dfull)
    weighted = d_mixed * norm_local
    total = norm_total(jnp.sum(weighted * gated, 1))
    d_gated = weighted * inverse - gated * inverse**3 * (total / DI)[:, None]
    g_norm_gated = jnp.sum(d_mixed * gated * inverse, 0)
    d_ssm = d_gated * jax.nn.silu(gate_pre)
    d_gate = d_gated * ssm_out * silu_slope(gate_pre)
    d_value_act, d_step, g_bias, g_decay, g_skip, d_in_map, d_out_map = scan_pull(d_ssm)
    d_state_act = lax.psum_scatter(
        jnp.concatenate([d_in_map, d_out_map], 1).astype(jnp.bfloat16),
        "tensor",
        scatter_dimension=1,
        tiled=True,
    ).astype(jnp.float32)
    d_value, g_vkernel, g_voffset = value_pull(d_value_act)
    d_state, g_skernel, g_soffset = state_pull(d_state_act)
    low_gate = d_gate.astype(jnp.bfloat16)
    low_value = d_value.astype(jnp.bfloat16)
    low_state = d_state.astype(jnp.bfloat16)
    low_step = d_step.astype(jnp.bfloat16)
    d_normed = (
        times_back(low_gate, w_gate)
        + times_back(low_value, value_weight)
        + times_back(low_state, w_state)
        + times_back(low_step, w_step)
    )
    grads = (
        times_over(full, low_gate),
        times_over(full, low_value),
        times_over(full, low_state),
        times_over(full, low_step),
        g_out,
    )
    d_rows, g_norm = norm_pull(rows_out(d_normed))
    smalls = (
        g_norm,
        g_norm_gated,
        g_vkernel,
        g_voffset,
        g_skernel,
        g_soffset,
        g_bias,
        g_decay,
        g_skip,
    )
    grad, g_mixer, smalls = (grad + d_rows, grads, smalls)
    mixer_sums = (
        lax.psum_scatter(g_mixer[0], "dp", scatter_dimension=0, tiled=True),
        lax.psum_scatter(g_mixer[1], "dp", scatter_dimension=0, tiled=True),
        lax.psum_scatter(g_mixer[2], "dp", scatter_dimension=0, tiled=True),
        lax.psum_scatter(g_mixer[3], "dp", scatter_dimension=0, tiled=True),
        lax.psum_scatter(g_mixer[4], "dp", scatter_dimension=1, tiled=True),
        lax.psum_scatter(g_shared_one[0], "dp", scatter_dimension=0, tiled=True),
        lax.psum_scatter(g_shared_one[1], "dp", scatter_dimension=0, tiled=True),
        lax.psum_scatter(g_shared_one[2], "dp", scatter_dimension=1, tiled=True),
    )
    g_nmix, g_ngated, g_vkernel, g_voffset, g_skernel, g_soffset, g_bias, g_decay, g_skip = smalls
    summed = lax.psum(
        (
            g_router_one,
            g_router_two,
            g_nmix,
            g_nmoe_one,
            g_nattn,
            g_nmoe_two,
            widen(g_ngated, value_start, DI, 0),
            widen(g_vkernel, value_start, DI, 1),
            widen(g_voffset, value_start, DI, 0),
            widen(g_skernel, state_start, 2 * NS, 1),
            widen(g_soffset, state_start, 2 * NS, 0),
            widen(g_bias, head_start, MH, 0),
            widen(g_decay, head_start, MH, 0),
            widen(g_skip, head_start, MH, 0),
        ),
        ("dp", "tensor"),
    )
    return (
        block_out,
        grad,
        mixer_sums[0],
        mixer_sums[1],
        mixer_sums[2],
        mixer_sums[3],
        mixer_sums[4],
        attention_sums[0],
        attention_sums[1],
        attention_sums[2],
        attention_sums[3],
        mixer_sums[5],
        mixer_sums[6],
        mixer_sums[7],
        attention_sums[4],
        attention_sums[5],
        attention_sums[6],
        g_experts_one[0],
        g_experts_one[1],
        g_experts_one[2],
        g_experts_two[0],
        g_experts_two[1],
        g_experts_two[2],
        summed[0],
        summed[1],
        summed[2],
        summed[3],
        summed[4],
        summed[5],
        summed[6],
        summed[7],
        summed[8],
        summed[9],
        summed[10],
        summed[11],
        summed[12],
        summed[13],
    )


def solution(mesh):
    in_specs = (
        P(("dp", "tensor"), None),
        P(("dp", "tensor"), None),
        P("dp", None),
        P("dp", None),
        P("dp", "tensor"),
        P("dp", "tensor"),
        P("dp", "tensor"),
        P("dp", "tensor"),
        P("tensor", "dp"),
        P("dp", "tensor"),
        P("dp", "tensor"),
        P("dp", "tensor"),
        P("tensor", "dp"),
        P("dp", "tensor"),
        P("dp", "tensor"),
        P("tensor", "dp"),
        P("dp", "tensor"),
        P("dp", "tensor"),
        P("tensor", "dp"),
        P("dp", None, "tensor"),
        P("dp", None, "tensor"),
        P("dp", "tensor", None),
        P("dp", None, "tensor"),
        P("dp", None, "tensor"),
        P("dp", "tensor", None),
        P(),
        P(),
        P(),
        P(),
        P(),
        P(),
        P(),
        P(),
        P(),
        P(),
        P(),
        P(),
        P(),
        P(),
    )
    out_specs = (
        P(("dp", "tensor"), None),
        P(("dp", "tensor"), None),
        P("dp", "tensor"),
        P("dp", "tensor"),
        P("dp", "tensor"),
        P("dp", "tensor"),
        P("tensor", "dp"),
        P("dp", "tensor"),
        P("dp", "tensor"),
        P("dp", "tensor"),
        P("tensor", "dp"),
        P("dp", "tensor"),
        P("dp", "tensor"),
        P("tensor", "dp"),
        P("dp", "tensor"),
        P("dp", "tensor"),
        P("tensor", "dp"),
        P("dp", None, "tensor"),
        P("dp", None, "tensor"),
        P("dp", "tensor", None),
        P("dp", None, "tensor"),
        P("dp", None, "tensor"),
        P("dp", "tensor", None),
        P(),
        P(),
        P(),
        P(),
        P(),
        P(),
        P(),
        P(),
        P(),
        P(),
        P(),
        P(),
        P(),
        P(),
    )
    return jax.shard_map(body, mesh=mesh, in_specs=in_specs, out_specs=out_specs, check_vma=False)
```

profile of v0, /device:TPU:0, one launch (start us, length us, event | category | flops | bytes accessed | tf_op | source)
XLA Modules:
  0.0 3665.4 jit_solution(6738060861636599864)
XLA Ops:
  98.2 65.6 %while.75 = (s32[]{:T(128)}, f32[24,64,128]{2,1,0:T(8,128)S(1)}, f32[2,128,24,64]{1,3,2,0:T(8,128)}, f32[2,128,128,24]{2,1,3,0:T(8,128)}, f32[2,128,128]{1,2,0:T...) while((s32[]{:T(128)}, f32[24,64,128]{2,1,0:T(8,128)S(1)}, ...), condition=%wide.region_3.4_spmd.clone.clone, body=%wide.region_1.3_spmd.clone.clone.sunk | while | flops 937245696 | bytes 106123960 | solution.py:82
  232.3 142.0 %all_to_all.42 = bf16[16,128,1536]{2,1,0:T(8,128)(2,1)S(1)} all-to-all(bf16[16,128,1536]{2,1,0:T(8,128)(2,1)S(1)} %broadcast_select_fusion.4), channel_id=1, replica_groups=mesh['dp'=16,'tensor'=2] {'dp'}, dimensions={0} | all-to-all | bytes 12582912 | tf_op jit(solution)/shard_map/all_to_all | solution.py:288
  394.9 99.6 %all-gather.19.cloned.1.call-done = bf16[1536,512]{1,0:T(8,128)(2,1)} async-done(((bf16[96,512]{1,0:T(8,128)(2,1)}), bf16[1536,512]{1,0:T(8,128)(2,1)}) %all-gather.19.cloned.1.call-update) | async-done | bytes 1572880 | tf_op jit(solution)/shard_map/all_gather | solution.py:235
  496.5 64.8 %all-gather.21.cloned.1.call-done = bf16[1536,512]{1,0:T(8,128)(2,1)} async-done(((bf16[96,512]{1,0:T(8,128)(2,1)}), bf16[1536,512]{1,0:T(8,128)(2,1)}) %all-gather.21.cloned.1.call-update) | async-done | bytes 1572880 | tf_op jit(solution)/shard_map/all_gather | solution.py:236
  683.4 34.9 all-gather.27.cloned.1.call-done
  824.7 140.6 %all_to_all.43 = bf16[16,128,1536]{2,1,0:T(8,128)(2,1)} all-to-all(bf16[16,128,1536]{2,1,0:T(8,128)(2,1)S(1)} %get-tuple-element.1853), channel_id=1, replica_groups=mesh['dp'=16,'tensor'=2] {'dp'}, dimensions={0} | all-to-all | bytes 12582912 | tf_op jit(solution)/shard_map/all_to_all | solution.py:288
  980.4 104.9 %all-to-all-done.4 = bf16[16,128,1536]{2,1,0:T(8,128)(2,1)} async-done(((bf16[16,128,1536]{2,1,0:T(8,128)(2,1)}), bf16[16,128,1536]{2,1,0:T(8,128)(2,1)}, u32[]{:S(2)}, u32[]{:S(2)}) %all-to-all-start.4) | async-done | bytes 6291488 | tf_op jit(solution)/shard_map/all_to_all | solution.py:346
  1098.2 28.2 all-to-all-start.3
  1133.3 116.8 %all-to-all-done.3 = bf16[16,128,1536]{2,1,0:T(8,128)(2,1)} async-done(((bf16[16,128,1536]{2,1,0:T(8,128)(2,1)}), bf16[16,128,1536]{2,1,0:T(8,128)(2,1)}, u32[]{:S(2)}, u32[]{:S(2)}) %all-to-all-start.3) | async-done | bytes 6291488 | tf_op jit(solution)/shard_map/all_to_all | solution.py:263
  1250.1 28.1 all-to-all-start.5
  1283.4 104.0 %all-gather.29.cloned.1.call-done = bf16[1536,512]{1,0:T(8,128)(2,1)} async-done(((bf16[96,512]{1,0:T(8,128)(2,1)}), bf16[1536,512]{1,0:T(8,128)(2,1)}) %all-gather.29.cloned.1.call-update) | async-done | bytes 1572880 | tf_op jit(solution)/shard_map/all_gather | solution.py:246
  1389.3 50.5 %all-gather.33.cloned.1.call-done = bf16[512,1536]{0,1:T(8,128)(2,1)} async-done(((bf16[512,96]{0,1:T(8,128)(2,1)}), bf16[512,1536]{0,1:T(8,128)(2,1)}) %all-gather.33.cloned.1.call-update) | async-done | bytes 1572880 | tf_op jit(solution)/shard_map/all_gather | solution.py:248
  1680.8 142.9 %all_to_all.44 = bf16[16,128,1536]{2,1,0:T(8,128)(2,1)S(1)} all-to-all(bf16[16,128,1536]{2,1,0:T(8,128)(2,1)S(1)} %broadcast_select_fusion.3), channel_id=1, replica_groups=mesh['dp'=16,'tensor'=2] {'dp'}, dimensions={0} | all-to-all | bytes 12582912 | tf_op jit(solution)/shard_map/all_to_all | solution.py:346
  1852.3 100.1 %all-to-all-done.7 = bf16[16,128,1536]{2,1,0:T(8,128)(2,1)} async-done(((bf16[16,128,1536]{2,1,0:T(8,128)(2,1)}), bf16[16,128,1536]{2,1,0:T(8,128)(2,1)}, u32[]{:S(2)}, u32[]{:S(2)}) %all-to-all-start.7) | async-done | bytes 6291488 | tf_op jit(solution)/shard_map/all_to_all | solution.py:263
  2002.6 39.0 %reduce-scatter.47.cloned.1.call-done = bf16[128,1536]{1,0:T(8,128)(2,1)} async-done(((bf16[256,1536]{1,0:T(8,128)(2,1)}), bf16[128,1536]{1,0:T(8,128)(2,1)}) %reduce-scatter.47.cloned.1.call-update) | async-done | bytes 393232 | tf_op jit(solution)/shard_map/reduce_scatter | solution.py:371
  2081.3 77.7 %while.76 = (s32[]{:T(128)}, f32[24]{0:T(128)}, f32[24,64,128]{2,1,0:T(8,128)S(1)}, f32[2,128,24,64]{1,3,2,0:T(8,128)}, f32[2,128,24]{2,1,0:T(8,128)}, /*index=5...) while((s32[]{:T(128)}, f32[24]{0:T(128)}, ...), condition=%wide.region_63.64_spmd.clone.clone, body=%wide.region_52.63_spmd.clone.clone.sunk | while | flops 1870191616 | bytes 48238296 | solution.py:82
  2272.4 57.9 %reduce-scatter.73.cloned.1.call-done = f32[96,512]{1,0:T(8,128)} async-done(((f32[1536,512]{1,0:T(8,128)}), f32[96,512]{1,0:T(8,128)}) %reduce-scatter.73.cloned.1.call-update) | async-done | bytes 196624 | tf_op jit(solution)/shard_map/reduce_scatter | solution.py:542
  2330.3 70.0 %reduce-scatter.75.cloned.1.call-done = f32[96,512]{1,0:T(8,128)} async-done(((f32[1536,512]{1,0:T(8,128)}), f32[96,512]{1,0:T(8,128)}) %reduce-scatter.75.cloned.1.call-update) | async-done | bytes 196624 | tf_op jit(solution)/shard_map/reduce_scatter | solution.py:543
  2400.3 69.9 %reduce-scatter.77.cloned.1.call-done = f32[512,96]{0,1:T(8,128)} async-done(((f32[512,1536]{0,1:T(8,128)}), f32[512,96]{0,1:T(8,128)}) %reduce-scatter.77.cloned.1.call-update) | async-done | bytes 196624 | tf_op jit(solution)/shard_map/reduce_scatter | solution.py:544
  2470.2 129.9 %all-reduce.27.cloned.1.call-done = (f32[1536,16]{0,1:T(8,128)}, f32[1536,16]{0,1:T(8,128)}) async-done(((f32[1536,16]{0,1:T(8,128)}, f32[1536,16]{0,1:T(8,128)}), (f32[1536,16]{0,1:T(8,128)}, f32[1536,16]{0,1:T(8,128)})) %all-reduce.27.cloned.1.call-update) | async-done | bytes 196624 | tf_op jit(solution)/shard_map/psum | solution.py:622
  2600.1 65.1 %reduce-scatter.63.cloned.1.call-done = f32[96,256]{1,0:T(8,128)} async-done(((f32[1536,256]{1,0:T(8,128)}), f32[96,256]{1,0:T(8,128)}) %reduce-scatter.63.cloned.1.call-update) | async-done | bytes 98320 | tf_op jit(solution)/shard_map/reduce_scatter | solution.py:540
  2665.2 62.8 %reduce-scatter.61.cloned.1.call-done = f32[96,256]{1,0:T(8,128)} async-done(((f32[1536,256]{1,0:T(8,128)}), f32[96,256]{1,0:T(8,128)}) %reduce-scatter.61.cloned.1.call-update) | async-done | bytes 98320 | tf_op jit(solution)/shard_map/reduce_scatter | solution.py:539
  2728.0 70.0 %reduce-scatter.67.cloned.1.call-done = f32[96,512]{1,0:T(8,128)} async-done(((f32[1536,512]{1,0:T(8,128)}), f32[96,512]{1,0:T(8,128)}) %reduce-scatter.67.cloned.1.call-update) | async-done | bytes 196624 | tf_op jit(solution)/shard_map/reduce_scatter | solution.py:617
  2797.9 70.0 %reduce-scatter.69.cloned.1.call-done = f32[96,512]{1,0:T(8,128)} async-done(((f32[1536,512]{1,0:T(8,128)}), f32[96,512]{1,0:T(8,128)}) %reduce-scatter.69.cloned.1.call-update) | async-done | bytes 196624 | tf_op jit(solution)/shard_map/reduce_scatter | solution.py:618
  2867.9 70.0 %reduce-scatter.71.cloned.1.call-done = f32[512,96]{0,1:T(8,128)} async-done(((f32[512,1536]{0,1:T(8,128)}), f32[512,96]{0,1:T(8,128)}) %reduce-scatter.71.cloned.1.call-update) | async-done | bytes 196624 | tf_op jit(solution)/shard_map/reduce_scatter | solution.py:619
  2937.9 79.2 %reduce-scatter.59.cloned.1.call-done = f32[96,768]{1,0:T(8,128)} async-done(((f32[1536,768]{1,0:T(8,128)}), f32[96,768]{1,0:T(8,128)}) %reduce-scatter.59.cloned.1.call-update) | async-done | bytes 294928 | tf_op jit(solution)/shard_map/reduce_scatter | solution.py:538
  3017.1 79.1 %reduce-scatter.65.cloned.1.call-done = f32[768,96]{0,1:T(8,128)} async-done(((f32[768,1536]{0,1:T(8,128)}), f32[768,96]{0,1:T(8,128)}) %reduce-scatter.65.cloned.1.call-update) | async-done | bytes 294928 | tf_op jit(solution)/shard_map/reduce_scatter | solution.py:541
  3096.2 60.1 %reduce-scatter.55.cloned.1.call-done = f32[96,128]{1,0:T(8,128)} async-done(((f32[1536,128]{1,0:T(8,128)}), f32[96,128]{1,0:T(8,128)}) %reduce-scatter.55.cloned.1.call-update) | async-done | bytes 49168 | tf_op jit(solution)/shard_map/reduce_scatter | solution.py:614
  3156.3 134.6 %all-reduce.25.cloned.1.call-done = (f32[1536]{0:T(1024)}, f32[1536]{0:T(1024)}, f32[1536]{0:T(1024)}, f32[1536]{0:T(1024)}, f32[3072]{0:T(1024)}, /*index=5*/f3...) async-done(((f32[1536]{0:T(1024)}, f32[1536]{0:T(1024)}, f32[1536]{0:T(1024)}, ...) | async-done | bytes 104016 | tf_op jit(solution)/shard_map/psum | solution.py:622
  3290.9 117.2 %reduce-scatter.57.cloned.1.call-done = f32[1536,96]{0,1:T(8,128)} async-done(((f32[1536,1536]{0,1:T(8,128)}), f32[1536,96]{0,1:T(8,128)}) %reduce-scatter.57.cloned.1.call-update) | async-done | bytes 589840 | tf_op jit(solution)/shard_map/reduce_scatter | solution.py:616
  3408.1 115.8 %reduce-scatter.53.cloned.1.call-done = f32[96,1536]{1,0:T(8,128)} async-done(((f32[1536,1536]{1,0:T(8,128)}), f32[96,1536]{1,0:T(8,128)}) %reduce-scatter.53.cloned.1.call-update) | async-done | bytes 589840 | tf_op jit(solution)/shard_map/reduce_scatter | solution.py:613
  3523.9 116.2 %reduce-scatter.51.cloned.1.call-done = f32[96,1536]{1,0:T(8,128)} async-done(((f32[1536,1536]{1,0:T(8,128)}), f32[96,1536]{1,0:T(8,128)}) %reduce-scatter.51.cloned.1.call-update) | async-done | bytes 589840 | tf_op jit(solution)/shard_map/reduce_scatter | solution.py:612
  (1068 shorter events, 1083.2 us)
Async XLA Ops:
  8.0 163.5 %all-gather.15.cloned.1.call-start = ((), (), s32[]{:S(2)}) async-start(), calls=%async_computation.35 | async-start | bytes 5013504 | tf_op jit(solution)/shard_map/all_gather | solution.py:230
  8.8 174.8 %all-gather.17.cloned.1.call-start = ((), (), s32[]{:S(2)}) async-start(), calls=%async_computation.36 | async-start | bytes 5013504 | tf_op jit(solution)/shard_map/all_gather | solution.py:234
  9.5 198.0 %reduce-scatter.35.cloned.1.call-start = ((), (), s32[]{:S(2)}) async-start(), calls=%async_computation.37 | async-start | bytes 1179648 | tf_op jit(solution)/shard_map/reduce_scatter | solution.py:255
  385.6 178.5 %all-to-all-start.1 = ((bf16[16,128,1536]{2,1,0:T(8,128)(2,1)}), bf16[16,128,1536]{2,1,0:T(8,128)(2,1)}, u32[]{:S(2)}, u32[]{:S(2)}) async-start(bf16[16,128,1536]{2,1,0:T(8,128)(2,1)} %convolution_convert_fusion.1), calls=%async_computation.2 | async-start | bytes 12582912 | tf_op jit(solution)/shard_map/all_to_all | solution.py:263
  391.9 169.4 %all-gather.21.cloned.1.call-start = ((), (), s32[]{:S(2)}) async-start(), calls=%async_computation.39 | async-start | bytes 1671168 | tf_op jit(solution)/shard_map/all_gather | solution.py:236
  392.5 216.8 %all-gather.23.cloned.1.call-start = ((), (), s32[]{:S(2)}) async-start(), calls=%async_computation.40 | async-start | bytes 1671168 | tf_op jit(solution)/shard_map/all_gather | solution.py:237
  393.2 266.9 %reduce-scatter.37.cloned.1.call-start = ((), (), s32[]{:S(2)}) async-start(), calls=%async_computation.41 | async-start | bytes 1179648 | tf_op jit(solution)/shard_map/reduce_scatter | solution.py:255
  613.6 156.3 %reduce-scatter.39.cloned.1.call-start = ((), (), s32[]{:S(2)}) async-start(), calls=%async_computation.44 | async-start | bytes 1179648 | tf_op jit(solution)/shard_map/reduce_scatter | solution.py:255
  1098.2 151.9 %all-to-all-start.3 = ((bf16[16,128,1536]{2,1,0:T(8,128)(2,1)}), bf16[16,128,1536]{2,1,0:T(8,128)(2,1)}, u32[]{:S(2)}, u32[]{:S(2)}) async-start(bf16[16,128,1536]{2,1,0:T(8,128)(2,1)} %convolution_convert_fusion), calls=%async_computation.6 | async-start | bytes 12582912 | tf_op jit(solution)/shard_map/all_to_all | solution.py:263
  1126.4 155.0 %all-gather.31.cloned.1.call-start = ((), (), s32[]{:S(2)}) async-start(), calls=%async_computation.46 | async-start | bytes 1671168 | tf_op jit(solution)/shard_map/all_gather | solution.py:247
  1250.1 241.3 %all-to-all-start.5 = ((bf16[16,128,1536]{2,1,0:T(8,128)(2,1)}), bf16[16,128,1536]{2,1,0:T(8,128)(2,1)}, u32[]{:S(2)}, u32[]{:S(2)}) async-start(bf16[16,128,1536]{2,1,0:T(8,128)(2,1)} %add_convert_fusion.1), calls=%async_computation.9 | async-start | bytes 12582912 | tf_op jit(solution)/shard_map/all_to_all | solution.py:263
  1279.0 160.8 %all-gather.33.cloned.1.call-start = ((), (), s32[]{:S(2)}) async-start(), calls=%async_computation.47 | async-start | bytes 1671168 | tf_op jit(solution)/shard_map/all_gather | solution.py:248
  1279.6 260.8 %reduce-scatter.79.cloned.1.call-start = ((), (), s32[]{:S(2)}) async-start(), calls=%async_computation.67 | async-start | bytes 98304
  1838.2 163.5 %reduce-scatter.81.cloned.1.call-start = ((), (), s32[]{:S(2)}) async-start(), calls=%async_computation.68 | async-start | bytes 98304
  1847.5 194.1 %reduce-scatter.47.cloned.1.call-start = ((), (), s32[]{:S(2)}) async-start(), calls=%async_computation.51 | async-start | bytes 1179648 | tf_op jit(solution)/shard_map/reduce_scatter | solution.py:371
  2001.5 177.0 %reduce-scatter.83.cloned.1.call-start = ((), (), s32[]{:S(2)}) async-start(), calls=%async_computation.69 | async-start | bytes 196608
  2183.4 146.9 %reduce-scatter.73.cloned.1.call-start = ((), (), s32[]{:S(2)}) async-start(), calls=%async_computation.64 | async-start | bytes 3342336 | tf_op jit(solution)/shard_map/reduce_scatter | solution.py:542
  2185.7 214.6 %reduce-scatter.75.cloned.1.call-start = ((), (), s32[]{:S(2)}) async-start(), calls=%async_computation.65 | async-start | bytes 3342336 | tf_op jit(solution)/shard_map/reduce_scatter | solution.py:543
  2188.9 281.2 %reduce-scatter.77.cloned.1.call-start = ((), (), s32[]{:S(2)}) async-start(), calls=%async_computation.66 | async-start | bytes 3342336 | tf_op jit(solution)/shard_map/reduce_scatter | solution.py:544
  2192.4 407.7 %all-reduce.27.cloned.1.call-start = ((), (), s32[]{:S(2)}) async-start(), calls=%async_computation.72 | async-start | bytes 393216 | tf_op jit(solution)/shard_map/psum | solution.py:622
  2194.7 470.5 %reduce-scatter.63.cloned.1.call-start = ((), (), s32[]{:S(2)}) async-start(), calls=%async_computation.59 | async-start | bytes 1671168 | tf_op jit(solution)/shard_map/reduce_scatter | solution.py:540
  2196.4 531.5 %reduce-scatter.61.cloned.1.call-start = ((), (), s32[]{:S(2)}) async-start(), calls=%async_computation.58 | async-start | bytes 1671168 | tf_op jit(solution)/shard_map/reduce_scatter | solution.py:539
  2198.1 599.8 %reduce-scatter.67.cloned.1.call-start = ((), (), s32[]{:S(2)}) async-start(), calls=%async_computation.61 | async-start | bytes 3342336 | tf_op jit(solution)/shard_map/reduce_scatter | solution.py:617
  2200.5 667.4 %reduce-scatter.69.cloned.1.call-start = ((), (), s32[]{:S(2)}) async-start(), calls=%async_computation.62 | async-start | bytes 3342336 | tf_op jit(solution)/shard_map/reduce_scatter | solution.py:618
  2203.8 734.0 %reduce-scatter.71.cloned.1.call-start = ((), (), s32[]{:S(2)}) async-start(), calls=%async_computation.63 | async-start | bytes 3342336 | tf_op jit(solution)/shard_map/reduce_scatter | solution.py:619
  2207.3 809.8 %reduce-scatter.59.cloned.1.call-start = ((), (), s32[]{:S(2)}) async-start(), calls=%async_computation.57 | async-start | bytes 5013504 | tf_op jit(solution)/shard_map/reduce_scatter | solution.py:538
  2211.2 885.0 %reduce-scatter.65.cloned.1.call-start = ((), (), s32[]{:S(2)}) async-start(), calls=%async_computation.60 | async-start | bytes 5013504 | tf_op jit(solution)/shard_map/reduce_scatter | solution.py:541
  2215.6 940.7 %reduce-scatter.55.cloned.1.call-start = ((), (), s32[]{:S(2)}) async-start(), calls=%async_computation.55 | async-start | bytes 835584 | tf_op jit(solution)/shard_map/reduce_scatter | solution.py:614
  2217.1 1073.8 %all-reduce.25.cloned.1.call-start = ((), (), s32[]{:S(2)}) async-start(), calls=%async_computation.71 | async-start | bytes 226304 | tf_op jit(solution)/shard_map/psum | solution.py:622
  2221.1 1187.0 %reduce-scatter.57.cloned.1.call-start = ((), (), s32[]{:S(2)}) async-start(), calls=%async_computation.56 | async-start | bytes 10027008 | tf_op jit(solution)/shard_map/reduce_scatter | solution.py:616
  2227.8 1296.1 %reduce-scatter.53.cloned.1.call-start = ((), (), s32[]{:S(2)}) async-start(), calls=%async_computation.54 | async-start | bytes 10027008 | tf_op jit(solution)/shard_map/reduce_scatter | solution.py:613
  2233.9 1406.2 %reduce-scatter.51.cloned.1.call-start = ((), (), s32[]{:S(2)}) async-start(), calls=%async_computation.53 | async-start | bytes 10027008 | tf_op jit(solution)/shard_map/reduce_scatter | solution.py:612
  (283 other events, 9231.0 us)
Sparse Core Ops, SparseCore 0:
  10.4 59.8 all-gather.12
  72.5 51.7 all-gather.14
  126.6 51.7 all-gather.16
  394.4 100.0 all-gather.18
  496.9 64.3 all-gather.20
  563.8 38.5 all-gather.22
  631.1 43.8 all-gather.24
  677.1 41.0 all-gather.26
  1129.5 106.0 all-gather.30
  1281.6 105.6 all-gather.28
  1389.8 50.0 all-gather.32
  1540.3 17.9 reduce-scatter.42
  1585.6 17.4 reduce-scatter.44
  2001.7 39.8 reduce-scatter.46
  2182.1 17.4 reduce-scatter.48
  2203.8 56.5 reduce-scatter.84
  2265.1 65.2 reduce-scatter.72
  2335.2 65.1 reduce-scatter.74
  2405.0 65.1 reduce-scatter.76
  2477.7 122.3 all-reduce.26
  2604.8 60.3 reduce-scatter.62
  2669.4 58.4 reduce-scatter.60
  2732.7 65.2 reduce-scatter.66
  2802.8 65.0 reduce-scatter.68
  2872.8 65.0 reduce-scatter.70
  2942.6 74.4 reduce-scatter.58
  3021.5 74.5 reduce-scatter.64
  3100.7 55.5 reduce-scatter.54
  3163.7 127.1 all-reduce.24
  3296.0 112.1 reduce-scatter.56
  3412.8 111.0 reduce-scatter.52
  3529.0 111.1 reduce-scatter.50
  (7 shorter events, 96.2 us)
where the time goes:
time: 3680 us; the launch traced here: 3670 us
  waiting for transfers between devices  2140 us (58%)
  blocking collectives  620 us (17%)
  local copies, waits for them, and re-layouts  361 us (10%)
  matrix products  255 us (7%)
  other arithmetic  197 us (5%)
  starting transfers between devices  76.8 us (2%)
    all_to_all x2, blocking collectives, moe_forward(): lax.all_to_all(taken, 'dp', split_axis=0, concat_axis=0, tiled=True)  283 us
    psum x2, waiting for transfers between devices, body(): lax.psum((g_router_one, g_router_two, g_nmix, g_nmoe_one, g_nattn, g_nmoe...  264 us
    all_to_all x4, waiting for transfers between devices, send_back(): lax.all_to_all(value_rows.astype(jnp.bfloat16), 'dp', split_axis=0, conca...  217 us
    all_to_all x1, blocking collectives, moe_backward(): lax.all_to_all(d_taken, 'dp', split_axis=0, concat_axis=0, tiled=True)  143 us
    reduce_scatter x1, waiting for transfers between devices, body(): lax.psum_scatter(g_mixer[4], 'dp', scatter_dimension=1, tiled=True)  117 us
    reduce_scatter x1, waiting for transfers between devices, body(): lax.psum_scatter(g_mixer[0], 'dp', scatter_dimension=0, tiled=True)  116 us
    reduce_scatter x1, waiting for transfers between devices, body(): lax.psum_scatter(g_mixer[1], 'dp', scatter_dimension=0, tiled=True)  116 us
    all_to_all x1, waiting for transfers between devices, moe_backward(): lax.all_to_all(d_taken, 'dp', split_axis=0, concat_axis=0, tiled=True)  105 us
  transfers between devices with their start and end apart: 44, of which 29 were waited for; matrix products, arithmetic and copies ran while one was open for 14% of the time, Pallas kernels for 0%

commit v1 on v0

v1 whole, which is shorter than its diff:
```python
import jax
import jax.numpy as jnp
from jax import lax
from jax.sharding import PartitionSpec as P

MH = 48
NS = 128
CH = 128
QUERY_HEADS = 12
KEY_VALUE_HEADS = 4
HEAD_SIZE = 128
TOP = 6
LEN = 256
DI = 3072


EPS = 1e-05
HIGH = lax.Precision.HIGHEST


def matmul(left, right):
    return jnp.dot(left, right, preferred_element_type=jnp.float32)


def times_back(left, right):
    return lax.dot_general(
        left, right, (((1,), (1,)), ((), ())), preferred_element_type=jnp.float32
    )


def times_over(left, right):
    return lax.dot_general(
        left, right, (((0,), (0,)), ((), ())), preferred_element_type=jnp.float32
    )


def rms_norm(value_rows, gain):
    return value_rows * lax.rsqrt(jnp.mean(value_rows * value_rows, -1, keepdims=True) + EPS) * gain


def causal_conv(value_rows, weight, bias):
    width = weight.shape[0]
    sequence_length = value_rows.shape[0]
    padded = jnp.concatenate(
        [jnp.zeros((width - 1, value_rows.shape[1]), jnp.float32), value_rows], 0
    )
    total = jnp.zeros_like(value_rows) + bias[None, :]
    for shift in range(width):
        total = total + weight[shift][None, :] * padded[shift : shift + sequence_length]
    return total


def conv_act(value_rows, weight, bias):
    return jax.nn.silu(causal_conv(value_rows, weight, bias))


def state_scan(heads_in, delta, rate, in_map, out_map):
    sequence_length, heads, width = heads_in.shape
    count = sequence_length // CH
    blocks = (
        heads_in.reshape(count, CH, heads, width),
        delta.reshape(count, CH, heads),
        in_map.reshape(count, CH, -1),
        out_map.reshape(count, CH, -1),
    )
    lower = (jnp.arange(CH)[:, None] >= jnp.arange(CH)[None, :])[:, :, None]

    def advance(state, block):
        x_blk, d_blk, b_blk, c_blk = block
        cum = jnp.cumsum(d_blk * rate[None, :], 0)
        diff = jnp.where(lower, cum[:, None, :] - cum[None, :, :], 0.0)
        decay = jnp.where(lower, jnp.exp(diff), 0.0)
        inner = jnp.dot(c_blk, b_blk.T, precision=HIGH)
        weights = inner[:, :, None] * decay * d_blk[None, :, :]
        local = jnp.einsum("ijh,jhp->ihp", weights, x_blk, precision=HIGH)
        carried = jnp.exp(cum)[:, :, None] * jnp.einsum("in,hpn->ihp", c_blk, state, precision=HIGH)
        tail = jnp.exp(cum[-1][None, :] - cum) * d_blk
        update = jnp.einsum("jhp,jn->hpn", tail[:, :, None] * x_blk, b_blk, precision=HIGH)
        return (jnp.exp(cum[-1])[:, None, None] * state + update, local + carried)

    start = jnp.zeros((heads, width, in_map.shape[1]), jnp.float32)
    outs, state = [], start
    for at in range(count):
        state, out = advance(state, tuple(block[at] for block in blocks))
        outs.append(out)
    return jnp.concatenate(outs, 0)


def scan_part(value_act, step_pre, step_bias, decay_log, skip_gain, in_map, out_map):
    sequence_length = value_act.shape[0]
    heads = step_pre.shape[1]
    heads_in = value_act.reshape(sequence_length, heads, -1)
    delta = jax.nn.softplus(step_pre + step_bias[None, :])
    rate = -jnp.exp(decay_log)
    outs = state_scan(heads_in, delta, rate, in_map, out_map) + skip_gain[None, :, None] * heads_in
    return outs.reshape(sequence_length, -1)


def silu_slope(value_rows):
    sig = jax.nn.sigmoid(value_rows)
    return sig * (1.0 + value_rows * (1.0 - sig))


AXES = ("dp", "tensor")
SPARE = 128
MOST_ROWS = 4096


def total_of(left, right):
    return left.astype(jnp.float32) + right.astype(jnp.float32)


def low(value_rows):
    return value_rows.astype(jnp.bfloat16)


def together(values):
    return lax.optimization_barrier(values)


def after(value, *others):
    return lax.optimization_barrier((value, others))[0]


class Grid:
    def __init__(self):
        self.dp = lax.axis_size("dp")
        self.nt = lax.axis_size("tensor")
        self.nc = 2
        self.na = 4
        self.nb = self.dp // (self.na * self.nc)
        index = lax.axis_index("dp")
        self.index = index
        self.c = index % self.nc
        self.b = (index // self.nc) % self.nb
        self.a = index // (self.nc * self.nb)
        self.t = lax.axis_index("tensor")
        self.step_t = (1, self.nt)
        self.step_c = (self.nt, self.nc)
        self.step_b = (self.nt * self.nc, self.nb)
        self.step_a = (self.nt * self.nc * self.nb, self.na)

    def shift(self, value, step, amount):
        stride, size = step
        pairs = []
        for source in range(self.dp * self.nt):
            digit = (source // stride) % size
            pairs.append((source, source + ((digit + amount) % size - digit) * stride))
        return lax.ppermute(value, AXES, pairs)

    def around(self, value, step):
        held = [value]
        for _ in range(step[1] - 1):
            held.append(self.shift(held[-1], step, 1))
        return held

    def sum_around(self, part, step):
        size = step[1]
        held = part(size - 1)
        for k in range(size - 2, -1, -1):
            held = total_of(part(k), self.shift(low(held), step, -1))
        return held

    def rounds(self, value):
        for k in range(self.na):
            ahead = self.shift(value, self.step_a, 1) if k < self.na - 1 else None
            near = self.around(value, self.step_b)
            if ahead is not None:
                ahead, near = together((ahead, near))
            yield near
            value = ahead

    def nearby(self):
        return [
            [
                (((self.a - k) % self.na) * self.nb + (self.b - kb) % self.nb) * self.nc
                + (self.c - kc) % self.nc
                for kc in range(self.nc)
                for kb in range(self.nb)
            ]
            for k in range(self.na)
        ]

    def with_core(self, near):
        return jnp.concatenate(near + [self.shift(block, self.step_c, 1) for block in near], 0)

    def core_sum(self, value):
        half = value.shape[0] // 2
        return low(total_of(value[:half], self.shift(value[half:], self.step_c, 1)))

    def collect_rounds(self, parts):
        total = None
        for k in range(self.na - 1, -1, -1):
            part = parts[k]
            count = part.shape[0] // self.nb
            if total is not None:
                part, total = together((part, low(total)))
                moved = self.shift(total, self.step_a, -1)
            near = self.sum_around(lambda kb: part[kb * count : (kb + 1) * count], self.step_b)
            if total is not None:
                near, moved = together((near, moved))
                near = total_of(near, moved)
            total = near
        return total

    def in_turn(self, step, value, rest, collect=None):
        if self.dp * value.shape[0] > MOST_ROWS:

            def near_of(held):
                return self.around(held, self.step_b)

            def advance(carry, item):
                held, total = carry
                part, *others = step(near_of(held), item)
                if collect is not None:
                    total = [old + new for old, new in zip(total, collect(item, others))]
                    others = []
                return (self.shift(held, self.step_a, 1), total), (part, others)

            total = []
            if collect is not None:
                item = tuple(leaf[0] for leaf in rest)
                shapes = jax.eval_shape(
                    lambda *args: collect(args[1], step(near_of(args[0]), args[1])[1:]), value, item
                )
                total = [jnp.zeros(shape.shape, jnp.float32) for shape in shapes]
            (_, total), (parts, others) = lax.scan(advance, (value, total), rest)
            others = others if collect is None else total
        else:
            results = [
                step(near, tuple(leaf[k] for leaf in rest))
                for k, near in enumerate(self.rounds(value))
            ]
            parts, *others = [list(leaves) for leaves in zip(*results)]
            if collect is not None:
                rows = [jnp.concatenate(list(leaf), 0) for leaf in rest]
                others = collect(rows, [jnp.concatenate(leaf, 0) for leaf in others])
        return self.collect_rounds(parts), others

    def gather_weight(self, value):
        held = []
        for near in self.rounds(value):
            held.extend(near)
        return self.with_core(held)

    def order(self, rows):
        at = jnp.arange(self.dp * rows, dtype=jnp.int32)
        kc, ka, kb = (
            at // (rows * self.nb * self.na),
            (at // (rows * self.nb)) % self.na,
            (at // rows) % self.nb,
        )
        a, b, c = (self.a - ka) % self.na, (self.b - kb) % self.nb, (self.c - kc) % self.nc
        source = ((a * self.nb + b) * self.nc + c) * rows + at % rows
        return low(jnp.arange(self.dp * rows, dtype=jnp.int32)[:, None] == source[None, :])

    def all_sum(self, value):
        half = value.shape[0] // 2
        keep = lax.dynamic_slice_in_dim(value, self.c * half, half, 0)
        send = lax.dynamic_slice_in_dim(value, (1 - self.c) * half, half, 0)
        value = keep + self.shift(send, self.step_c, 1)
        for step in (self.step_t, self.step_b, self.step_a):
            value = sum(self.around(value, step))
        other = self.shift(value, self.step_c, 1)
        return jnp.where(
            self.c == 0,
            jnp.concatenate([value, other], 0),
            jnp.concatenate([other, value], 0),
        )

    def scatter_weight(self, value):
        rows = value.shape[0] // self.dp
        parts = value.reshape(self.na * self.nb, self.nc, rows, -1)
        send = lax.dynamic_index_in_dim(parts, (self.c + 1) % self.nc, 1, keepdims=False)
        keep = lax.dynamic_index_in_dim(parts, self.c, 1, keepdims=False)
        both = low(total_of(keep, self.shift(send, self.step_c, 1)))

        def block(ka, kb):
            at = ((self.a - ka) % self.na) * self.nb + (self.b - kb) % self.nb
            return lax.dynamic_index_in_dim(both, at, 0, keepdims=False)

        return self.collect_rounds(
            [
                jnp.concatenate([block(ka, kb) for kb in range(self.nb)], 0)
                for ka in range(self.na)
            ]
        )

    def swap(self, value):
        return self.shift(value, self.step_t, 1)

    def pair_rows(self, value):
        other = self.swap(value)
        return jnp.where(
            self.t == 0,
            jnp.concatenate([value, other], 0),
            jnp.concatenate([other, value], 0),
        )

    def pair_sum(self, value, axis):
        half = value.shape[axis] // 2
        keep = lax.dynamic_slice_in_dim(value, self.t * half, half, axis)
        send = lax.dynamic_slice_in_dim(value, (1 - self.t) * half, half, axis)
        return total_of(keep, self.swap(low(send)))


def dense_gates(logits, picked):
    shown = jnp.where(picked, logits, -1e30)
    raised = jnp.where(picked, jnp.exp(logits - jnp.max(shown, 1, keepdims=True)), 0.0)
    return raised / jnp.sum(raised, 1, keepdims=True)


def body(
    hidden_in,
    out_grad,
    routes_first,
    routes_second,
    in_gate,
    in_value,
    in_state,
    in_step,
    mix_output,
    attn_query,
    attention_key_matrix,
    attention_value_matrix,
    attn_output,
    shared_gate_one,
    shared_up_one,
    shared_down_one,
    shared_gate_two,
    shared_up_two,
    shared_down_two,
    expert_gate_one,
    expert_up_one,
    expert_down_one,
    expert_gate_two,
    expert_up_two,
    expert_down_two,
    router_one,
    router_two,
    norm_mix,
    norm_moe_one,
    norm_attn,
    norm_moe_two,
    gated_norm,
    conv_value_weight,
    conv_value_bias,
    conv_state_weight,
    conv_state_bias,
    step_bias,
    decay_log,
    skip_gain,
):
    grid = Grid()
    tensor_rank = grid.t
    expert_count = grid.dp
    local_rows = hidden_in.shape[0]
    value_cols = in_value.shape[1]
    state_cols = in_state.shape[1]
    head_cols = in_step.shape[1]
    value_start = tensor_rank * value_cols
    state_start = tensor_rank * state_cols
    head_start = tensor_rank * head_cols
    norm_local = lax.dynamic_slice_in_dim(gated_norm, value_start, value_cols, 0)
    value_kernel = lax.dynamic_slice_in_dim(conv_value_weight, value_start, value_cols, 1)
    value_offset = lax.dynamic_slice_in_dim(conv_value_bias, value_start, value_cols, 0)
    state_kernel = lax.dynamic_slice_in_dim(conv_state_weight, state_start, state_cols, 1)
    state_offset = lax.dynamic_slice_in_dim(conv_state_bias, state_start, state_cols, 0)
    bias_local = lax.dynamic_slice_in_dim(step_bias, head_start, head_cols, 0)
    decay_local = lax.dynamic_slice_in_dim(decay_log, head_start, head_cols, 0)
    skip_local = lax.dynamic_slice_in_dim(skip_gain, head_start, head_cols, 0)
    scale = HEAD_SIZE ** (-0.5)
    model = hidden_in.shape[1]
    narrow = state_cols + head_cols
    block_rows = in_value.shape[0]

    rows = hidden_in.astype(jnp.float32)
    normalized_input, norm_pull = jax.vjp(rms_norm, rows, norm_mix)
    full = grid.pair_rows(low(normalized_input))
    sequence_length = full.shape[0]
    order = grid.order(block_rows)

    w_first = grid.gather_weight(
        jnp.concatenate(
            [in_value, in_state, in_step, jnp.zeros((block_rows, -narrow % 128), jnp.bfloat16)], 1
        )
    )
    value_weight = w_first[:, :value_cols]
    w_narrow = w_first[:, value_cols:]
    w_gate = grid.gather_weight(after(in_gate, w_first))
    w_out_t = grid.gather_weight(after(mix_output.T, w_gate))
    q_cols = attn_query.shape[1]
    k_cols = attention_key_matrix.shape[1]
    wide_cols = q_cols + 2 * k_cols

    shared_units = shared_gate_one.shape[1] // expert_count
    shared_parts = jnp.stack(
        [
            shared_gate_one,
            shared_up_one,
            shared_down_one.T,
            shared_gate_two,
            shared_up_two,
            shared_down_two.T,
        ],
        1,
    ).reshape(block_rows, 6, expert_count, shared_units)
    shared_parts = shared_parts.transpose(2, 0, 1, 3)
    shared_own = lax.all_to_all(
        after(shared_parts.reshape(expert_count, block_rows, 6 * shared_units), w_first),
        "dp",
        split_axis=0,
        concat_axis=0,
        tiled=True,
    ).reshape(model, 6 * shared_units)
    shared_other = grid.swap(shared_own)

    def shared_of(which):
        at = which * shared_units
        return [
            shared_own[:, at : at + shared_units],
            shared_other[:, at : at + shared_units],
        ]

    def expert_weights(bank, which, when):
        own = [leaf[0] for leaf in bank]
        gate_other, up_other, down_other = [grid.swap(leaf) for leaf in after(own, when)]
        gate_own, up_own, down_own = own
        w_in = jnp.concatenate(
            [gate_own, gate_other, up_own, up_other] + shared_of(which) + shared_of(which + 1), 1
        )
        down_t = jnp.concatenate(shared_of(which + 2), 1)
        w_down = jnp.concatenate([down_own, down_other, down_t.T], 0)
        return w_in, w_down

    experts_one = expert_weights((expert_gate_one, expert_up_one, expert_down_one), 0, full)
    half_units = expert_gate_one.shape[2]
    units = 2 * half_units
    pair_units = 2 * shared_units

    def local_mask(routes):
        mine = lax.dynamic_slice_in_dim(routes, tensor_rank * local_rows, local_rows, 0)
        names = jnp.arange(expert_count, dtype=jnp.int32)
        return jnp.any(mine[:, :, None] == names[None, None, :], 1)

    mask_one, mask_two = local_mask(routes_first), local_mask(routes_second)
    masks = lax.all_gather(low(jnp.concatenate([mask_one, mask_two], 1)), "dp", axis=0)
    masks = [
        jnp.concatenate([masks[at] for at in blocks], 0) > 0.5 for blocks in grid.nearby()
    ]
    picked_one = jnp.stack([mask[:, :expert_count] for mask in masks])
    picked_two = jnp.stack([mask[:, expert_count:] for mask in masks])
    here = (jnp.arange(expert_count, dtype=jnp.int32) == grid.index)[None, :]

    def split_up(before):
        wide = before.astype(jnp.float32)
        edges = [units, 2 * units, 2 * units + pair_units]
        return jnp.split(wide, edges, 1)

    def moe_forward(rows, gain, router, picked, weights):
        w_in, w_down = weights
        normalized_input, norm_pull = jax.vjp(rms_norm, rows, gain)
        local = low(normalized_input)

        def step(near, chunk):
            (chosen,) = chunk
            every = grid.with_core(near)
            gates = dense_gates(matmul(every, router), chosen)
            gate = jnp.sum(jnp.where(here, gates, 0.0), 1, keepdims=True)
            before = low(matmul(every, w_in))
            first, second, shared_a, shared_b = split_up(before)
            hidden = jnp.concatenate(
                [
                    low(jax.nn.silu(first) * second * gate),
                    low(jax.nn.silu(shared_a) * shared_b),
                ],
                1,
            )
            part = grid.core_sum(low(matmul(hidden, w_down)))
            return (part, every, gate, before, hidden)

        result, kept = grid.in_turn(step, local, (picked,))
        return (rows + result, (norm_pull, local, kept))

    def moe_backward(grad, router, local_picked, weights, keep):
        w_in, w_down = weights
        norm_pull, local, kept = keep
        spare = jnp.arange(SPARE, dtype=jnp.int32)[None, :] == grid.index

        def step(near, chunk):
            _, gate, before, _ = chunk
            d_every = grid.with_core(near)
            first, second, shared_a, shared_b = split_up(before)
            d_before = low(times_back(d_every, w_down)).astype(jnp.float32)
            d_hidden, d_shared = d_before[:, :units], d_before[:, units:]
            active = jax.nn.silu(first)
            d_gate = jnp.sum(d_hidden * active * second, 1, keepdims=True)
            d_hidden = d_hidden * gate
            d_in = jnp.concatenate(
                [
                    low(d_hidden * second * silu_slope(first)),
                    low(d_hidden * active),
                    low(d_shared * shared_b * silu_slope(shared_a)),
                    low(d_shared * jax.nn.silu(shared_a)),
                ],
                1,
            )
            d_in = together(d_in)
            sent = jnp.concatenate(
                [low(times_back(d_in, w_in)), low(jnp.where(spare, d_gate, 0.0))], 1
            )
            return (grid.core_sum(sent), d_every, d_in)

        def collect(chunk, more):
            every, _, _, hidden = chunk
            d_every, d_in = more
            return times_over(every, d_in), times_over(hidden, d_every)

        got, (g_in, g_down) = grid.in_turn(step, low(grad), kept, collect)
        own, other = slice(0, half_units), slice(half_units, units)
        own_up = slice(units, units + half_units)
        other_up = slice(units + half_units, 2 * units)
        g_experts = (
            (g_in[:, own] + grid.swap(low(g_in[:, other])))[None],
            (g_in[:, own_up] + grid.swap(low(g_in[:, other_up])))[None],
            (g_down[own] + grid.swap(low(g_down[other])))[None],
        )
        g_rest, g_rest_down = g_in[:, 2 * units :], g_down[units:].T
        s = shared_units
        mine = jnp.concatenate([g_rest[:, :s], g_rest[:, 2 * s : 3 * s], g_rest_down[:, :s]], 1)
        theirs = jnp.concatenate([g_rest[:, s : 2 * s], g_rest[:, 3 * s :], g_rest_down[:, s:]], 1)
        g_shared = low(mine + grid.swap(low(theirs)))
        gates = dense_gates(matmul(local, router), local_picked)
        d_gates = got[:, model : model + expert_count]
        d_logits = low(gates * (d_gates - jnp.sum(gates * d_gates, 1, keepdims=True)))
        d_local = got[:, :model] + times_back(d_logits, router)
        g_router = times_over(d_logits, local)
        d_rows, g_gain = norm_pull(d_local)
        return (grad + d_rows, g_gain, g_router, g_shared, g_experts)

    ordered = low(matmul(full, order))
    value_pre = matmul(ordered, value_weight)
    narrow_pre = matmul(ordered, w_narrow)
    state_pre = narrow_pre[:, :state_cols]
    step_pre = narrow_pre[:, state_cols:narrow]
    gate_pre = matmul(ordered, w_gate)
    value_act, value_pull = jax.vjp(conv_act, value_pre, value_kernel, value_offset)
    state_act, state_pull = jax.vjp(conv_act, state_pre, state_kernel, state_offset)
    state_own = low(state_act)
    state_other = grid.swap(state_own)
    in_map = jnp.where(tensor_rank == 0, state_own, state_other).astype(jnp.float32)
    out_map = jnp.where(tensor_rank == 0, state_other, state_own).astype(jnp.float32)
    ssm_out, scan_pull = jax.vjp(
        scan_part, value_act, step_pre, bias_local, decay_local, skip_local, in_map, out_map
    )
    gated = ssm_out * jax.nn.silu(gate_pre)
    square = jnp.sum(gated * gated, 1, keepdims=True)
    inverse = lax.rsqrt((square + grid.swap(square)) / DI + EPS)
    mixed = low(gated * inverse * norm_local)
    mixed_out = low(times_back(low(times_back(mixed, w_out_t)), order))
    result = rows + grid.pair_sum(mixed_out, 0)
    experts_two = expert_weights((expert_gate_two, expert_up_two, expert_down_two), 3, result)
    w_attention = lax.all_gather(
        after(
            jnp.concatenate(
                [attn_query, attention_key_matrix, attention_value_matrix, attn_output.T], 1
            ),
            w_out_t,
        ),
        "dp",
        axis=0,
        tiled=True,
    )
    qkv_weight = w_attention[:, :wide_cols]
    attn_out_t = w_attention[:, wide_cols:]
    state_two, moe_one_keep = moe_forward(result, norm_moe_one, router_one, picked_one, experts_one)

    normalized_input, attention_norm_pull = jax.vjp(rms_norm, state_two, norm_attn)
    attention_full = grid.pair_rows(low(normalized_input))
    kv_heads = k_cols // HEAD_SIZE
    query_groups = QUERY_HEADS // KEY_VALUE_HEADS
    qkv = low(matmul(attention_full, qkv_weight))
    query_rows = qkv[:, :q_cols].reshape(sequence_length, kv_heads, query_groups, HEAD_SIZE)
    key_rows = qkv[:, q_cols : q_cols + k_cols].reshape(sequence_length, kv_heads, HEAD_SIZE)
    value_rows = qkv[:, q_cols + k_cols :].reshape(sequence_length, kv_heads, HEAD_SIZE)
    causal = jnp.arange(sequence_length)[:, None] >= jnp.arange(sequence_length)[None, :]
    scores = (
        jnp.einsum("ikgd,jkd->kgij", query_rows, key_rows, preferred_element_type=jnp.float32)
        * scale
    )
    scores = jnp.where(causal, scores, -1e30)
    peak = jnp.max(scores, 3, keepdims=True)
    raised = jnp.exp(scores - peak)
    total = jnp.sum(raised, 3, keepdims=True)
    probs = raised / total
    low_probs = low(probs)
    attended = jnp.einsum(
        "kgij,jkd->ikgd", low_probs, value_rows, preferred_element_type=jnp.float32
    )
    attended = low(attended.reshape(sequence_length, -1))
    result = state_two + grid.pair_sum(times_back(attended, attn_out_t), 0)
    block_out, moe_two_keep = moe_forward(
        result, norm_moe_two, router_two, picked_two, experts_two
    )

    grad = out_grad.astype(jnp.float32)
    grad, g_nmoe_two, g_router_two, g_shared_two, g_experts_two = moe_backward(
        grad, router_two, mask_two, experts_two, moe_two_keep
    )

    dfull = grid.pair_rows(low(grad))
    d_att = low(matmul(dfull, attn_out_t)).reshape(query_rows.shape)
    g_out_t = low(times_over(dfull, attended))
    d_probs = jnp.einsum("ikgd,jkd->kgij", d_att, value_rows, preferred_element_type=jnp.float32)
    d_scores = low(probs * (d_probs - jnp.sum(probs * d_probs, 3, keepdims=True)))
    d_query = low(
        jnp.einsum("kgij,jkd->ikgd", d_scores, key_rows, preferred_element_type=jnp.float32) * scale
    ).reshape(sequence_length, -1)
    d_keys = low(
        jnp.einsum("kgij,ikgd->jkd", d_scores, query_rows, preferred_element_type=jnp.float32)
        * scale
    ).reshape(sequence_length, -1)
    d_values = low(
        jnp.einsum("kgij,ikgd->jkd", low_probs, d_att, preferred_element_type=jnp.float32)
    ).reshape(sequence_length, -1)
    d_qkv = jnp.concatenate([d_query, d_keys, d_values], 1)
    g_qkv = low(times_over(attention_full, d_qkv))
    d_rows, g_nattn = attention_norm_pull(grid.pair_sum(times_back(d_qkv, qkv_weight), 0))
    grad = grad + d_rows

    grad, g_nmoe_one, g_router_one, g_shared_one, g_experts_one = moe_backward(
        grad, router_one, mask_one, experts_one, moe_one_keep
    )

    attention_sum = grid.scatter_weight(after(jnp.concatenate([g_qkv, g_out_t], 1), grad))
    dfull = grid.pair_rows(low(grad))
    d_mixed = matmul(low(matmul(dfull, order)), w_out_t)
    mix_out_sum = grid.scatter_weight(after(low(times_over(dfull, mixed)), attention_sum))
    weighted = d_mixed * norm_local
    total = jnp.sum(weighted * gated, 1, keepdims=True)
    total = total + grid.swap(total)
    d_gated = weighted * inverse - gated * inverse**3 * (total / DI)
    g_ngated = jnp.sum(d_mixed * gated * inverse, 0)
    d_ssm = d_gated * jax.nn.silu(gate_pre)
    low_gate = low(d_gated * ssm_out * silu_slope(gate_pre))
    gate_sum = grid.scatter_weight(after(low(times_over(full, low_gate)), mix_out_sum))
    d_ssm = after(d_ssm, attention_sum)
    d_value_act, d_step, g_bias, g_decay, g_skip, d_in_map, d_out_map = scan_pull(d_ssm)
    map_keep = jnp.where(tensor_rank == 0, d_in_map, d_out_map)
    map_send = jnp.where(tensor_rank == 0, d_out_map, d_in_map)
    d_state_act = total_of(map_keep, grid.swap(low(map_send)))
    d_value, g_vkernel, g_voffset = value_pull(d_value_act)
    d_state, g_skernel, g_soffset = state_pull(d_state_act)
    low_value = after(low(d_value), gate_sum)
    low_narrow = jnp.concatenate(
        [low(d_state), low(d_step), jnp.zeros((sequence_length, -narrow % 128), jnp.bfloat16)], 1
    )
    d_normed = (
        times_back(low_gate, w_gate)
        + times_back(low_value, value_weight)
        + times_back(low_narrow, w_narrow)
    )
    value_sum = grid.scatter_weight(
        low(jnp.concatenate([times_over(full, low_value), times_over(full, low_narrow)], 1))
    )
    d_normed = times_back(low(d_normed), order)
    d_rows, g_nmix = norm_pull(grid.pair_sum(d_normed, 0))
    grad = grad + d_rows

    shared_grads = jnp.concatenate([g_shared_one, g_shared_two], 1)
    shared_back = lax.all_to_all(
        shared_grads.reshape(expert_count, block_rows, 6 * shared_units),
        "dp",
        split_axis=0,
        concat_axis=0,
        tiled=True,
    ).astype(jnp.float32)
    shared_back = shared_back.reshape(expert_count, block_rows, 6, shared_units)
    shared_back = shared_back.transpose(2, 1, 0, 3).reshape(6, block_rows, -1)

    def spread(value, start, whole):
        value = value.reshape(-1, value.shape[-1])
        wide = jnp.zeros((value.shape[0], whole), jnp.float32)
        return lax.dynamic_update_slice_in_dim(wide, value, start, 1).reshape(-1)

    def all_sums(pieces):
        sizes = [piece.size for piece in pieces]
        packed = [piece.reshape(-1) for piece in pieces]
        packed.append(jnp.zeros((-sum(sizes) % 2048,), jnp.float32))
        packed = grid.all_sum(jnp.concatenate(packed).reshape(-1, 128)).reshape(-1)
        summed, at = [], 0
        for size in sizes:
            summed.append(packed[at : at + size])
            at += size
        return summed

    summed = all_sums((g_router_one, g_router_two, g_nmoe_one, g_nattn, g_nmoe_two))
    summed = summed[:2] + all_sums((g_nmix,)) + summed[2:]
    summed += all_sums(
        (
            spread(g_ngated, value_start, DI),
            spread(g_vkernel, value_start, DI),
            spread(g_voffset, value_start, DI),
            spread(g_skernel, state_start, 2 * NS),
            spread(g_soffset, state_start, 2 * NS),
            spread(g_bias, head_start, MH),
            spread(g_decay, head_start, MH),
            spread(g_skip, head_start, MH),
        )
    )
    return (
        block_out,
        grad,
        gate_sum,
        value_sum[:, :value_cols],
        value_sum[:, value_cols : value_cols + state_cols],
        value_sum[:, value_cols + state_cols : value_cols + narrow],
        mix_out_sum.T,
        attention_sum[:, :q_cols],
        attention_sum[:, q_cols : q_cols + k_cols],
        attention_sum[:, q_cols + k_cols : wide_cols],
        attention_sum[:, wide_cols:].T,
        shared_back[0],
        shared_back[1],
        shared_back[2].T,
        shared_back[3],
        shared_back[4],
        shared_back[5].T,
        g_experts_one[0],
        g_experts_one[1],
        g_experts_one[2],
        g_experts_two[0],
        g_experts_two[1],
        g_experts_two[2],
        summed[0].reshape(expert_count, model).T,
        summed[1].reshape(expert_count, model).T,
        summed[2],
        summed[3],
        summed[4],
        summed[5],
        summed[6],
        summed[7].reshape(-1, DI),
        summed[8],
        summed[9].reshape(-1, 2 * NS),
        summed[10],
        summed[11],
        summed[12],
        summed[13],
    )


def solution(mesh):
    in_specs = (
        P(("dp", "tensor"), None),
        P(("dp", "tensor"), None),
        P("dp", None),
        P("dp", None),
        P("dp", "tensor"),
        P("dp", "tensor"),
        P("dp", "tensor"),
        P("dp", "tensor"),
        P("tensor", "dp"),
        P("dp", "tensor"),
        P("dp", "tensor"),
        P("dp", "tensor"),
        P("tensor", "dp"),
        P("dp", "tensor"),
        P("dp", "tensor"),
        P("tensor", "dp"),
        P("dp", "tensor"),
        P("dp", "tensor"),
        P("tensor", "dp"),
        P("dp", None, "tensor"),
        P("dp", None, "tensor"),
        P("dp", "tensor", None),
        P("dp", None, "tensor"),
        P("dp", None, "tensor"),
        P("dp", "tensor", None),
        P(),
        P(),
        P(),
        P(),
        P(),
        P(),
        P(),
        P(),
        P(),
        P(),
        P(),
        P(),
        P(),
        P(),
    )
    out_specs = (
        P(("dp", "tensor"), None),
        P(("dp", "tensor"), None),
        P("dp", "tensor"),
        P("dp", "tensor"),
        P("dp", "tensor"),
        P("dp", "tensor"),
        P("tensor", "dp"),
        P("dp", "tensor"),
        P("dp", "tensor"),
        P("dp", "tensor"),
        P("tensor", "dp"),
        P("dp", "tensor"),
        P("dp", "tensor"),
        P("tensor", "dp"),
        P("dp", "tensor"),
        P("dp", "tensor"),
        P("tensor", "dp"),
        P("dp", None, "tensor"),
        P("dp", None, "tensor"),
        P("dp", "tensor", None),
        P("dp", None, "tensor"),
        P("dp", None, "tensor"),
        P("dp", "tensor", None),
        P(),
        P(),
        P(),
        P(),
        P(),
        P(),
        P(),
        P(),
        P(),
        P(),
        P(),
        P(),
        P(),
        P(),
    )
    return jax.shard_map(body, mesh=mesh, in_specs=in_specs, out_specs=out_specs, check_vma=False)
```

time: 3680 us -> 1310 us (0.36)
  waiting for transfers between devices: 2140 us -> 497 us
  blocking collectives: 620 us -> 20.6 us
  local copies, waits for them, and re-layouts: 361 us -> 178 us
  starting transfers between devices: 76.8 us -> 231 us
  other arithmetic: 197 us -> 124 us
    reduce_scatter x22 -> x0, waiting for transfers between devices: 1190 us -> none  [the longest x1 117 us: body(): lax.psum_scatter(g_mixer[4], 'dp', scatter_dimension=1, tiled=True)]
    ppermute x0 -> x229, waiting for transfers between devices: none -> 497 us  [shift(): return lax.ppermute(value, AXES, pairs)]
    all_to_all x3 -> x0, blocking collectives: 425 us -> none  [the longest x2 283 us: moe_forward(): lax.all_to_all(taken, 'dp', split_axis=0, concat_axis=0, tiled=True)]
    all_gather x11 -> x1, waiting for transfers between devices: 355 us -> 0.01 us  [body(): lax.all_gather(after(jnp.concatenate([attn_query, attention_key_matrix, a...]
    all_to_all x5 -> x2, waiting for transfers between devices: 322 us -> 0.01 us  [the longest x1 0.01 us: body(): lax.all_to_all(after(shared_parts.reshape(expert_count, block_rows, 6 * s...]
    psum x2 -> x0, waiting for transfers between devices: 264 us -> none  [body(): lax.psum((g_router_one, g_router_two, g_nmix, g_nmoe_one, g_nattn, g_nmoe...]
    ppermute x0 -> x229, starting transfers between devices: none -> 220 us  [shift(): return lax.ppermute(value, AXES, pairs)]
    all_gather x13 -> x1, blocking collectives: 184 us -> 20.6 us  [body(): lax.all_gather(low(jnp.concatenate([mask_one, mask_two], 1)), 'dp', axis=0)]
  transfers between devices with their start and end apart: 44 -> 232, of which waited for: 29 -> 103; matrix products, arithmetic and copies ran while one was open for 14% -> 32% of each run, Pallas kernels for 0% -> 0%
where the time goes in v1:
time: 1310 us; the launch traced here: 1300 us
  waiting for transfers between devices  497 us (38%)
  starting transfers between devices  231 us (18%)
  matrix products  229 us (17%)
  local copies, waits for them, and re-layouts  178 us (14%)
  other arithmetic  124 us (9%)
  between operations  21.1 us (2%)
  blocking collectives  20.6 us (2%)
    ppermute x229, waiting for transfers between devices, shift(): return lax.ppermute(value, AXES, pairs)  497 us
    ppermute x229, starting transfers between devices, shift(): return lax.ppermute(value, AXES, pairs)  220 us
    dot_general x33, matrix products, matmul(): return jnp.dot(left, right, preferred_element_type=jnp.float32)  68.1 us
    dot_general x24, matrix products, times_back(): lax.dot_general(left, right, (((1,), (1,)), ((), ())), preferred_element_...  65.9 us
    unnamed x803, local copies, waits for them, and re-layouts  60.3 us
    dot_general x12, matrix products, times_over(): lax.dot_general(left, right, (((0,), (0,)), ((), ())), preferred_element_...  51.3 us
    convert_element_type x79, other arithmetic, low(): return value_rows.astype(jnp.bfloat16)  45.9 us
  transfers between devices with their start and end apart: 232, of which 103 were waited for; matrix products, arithmetic and copies ran while one was open for 32% of the time, Pallas kernels for 0%

profile of v1, /device:TPU:0, one launch (start us, length us, event | category | flops | bytes accessed | tf_op | source)
XLA Modules:
  0.0 1301.4 jit_solution(10088161046892008943)
XLA Ops:
  32.2 20.6 %all_gather.7 = bf16[16,128,32]{1,2,0:T(8,128)(2,1)S(1)} all-gather(bf16[1,128,32]{1,2,0:T(8,128)(2,1)S(1)} %add_convert_fusion.36), channel_id=1, replica_groups=mesh['dp'=16,'tensor'=2] {'dp'}, dimensions={0}, use_global_device_ids=true | all-gather | bytes 139264 | tf_op jit(solution)/shard_map/all_gather | solution.py:447
  102.7 7.4 collective-permute-done.7
  115.6 9.8 collective-permute-done.125
  179.9 7.8 collective-permute-done.19
  190.1 7.3 collective-permute-done.21
  198.1 8.8 collective-permute-done.23
  228.6 7.6 collective-permute-done.35
  247.3 7.9 collective-permute-done.39
  272.8 11.7 collective-permute-done.48
  303.9 9.8 collective-permute-done.58
  318.9 16.0 %collective-permute-done.63 = bf16[128,1536]{1,0:T(8,128)(2,1)S(1)} collective-permute-done((bf16[128,1536]{1,0:T(8,128)(2,1)S(1)}, bf16[128,1536]{1,0:T(8,128)(2,1)S(1)}, u32[]{:S(2)}, u32[]{:S(2)}) %collective-permute-start.63) | collective-permute-done | bytes 393248 | tf_op jit(solution)/shard_map/ppermute | solution.py:149
  367.0 10.7 collective-permute-done.72
  422.7 38.8 %collective-permute-done.87 = bf16[256,1536]{1,0:T(8,128)(2,1)} collective-permute-done((bf16[256,1536]{1,0:T(8,128)(2,1)}, bf16[256,1536]{1,0:T(8,128)(2,1)}, u32[]{:S(2)}, u32[]{:S(2)}) %collective-permute-start.87) | collective-permute-done | bytes 786464 | tf_op jit(solution)/shard_map/ppermute | solution.py:149
  549.8 12.6 fusion.548
  589.8 33.0 %collective-permute-done.201 = bf16[1536,96]{0,1:T(8,128)(2,1)S(1)} collective-permute-done((bf16[1536,96]{0,1:T(8,128)(2,1)S(1)}, bf16[1536,96]{0,1:T(8,128)(2,1)S(1)}, u32[]{:S(2)}, u32[]{:S(2)}) %collective-permute-start.201) | collective-permute-done | bytes 294944 | tf_op jit(solution)/shard_map/ppermute | solution.py:149
  631.6 9.0 collective-permute-done.103
  642.2 7.5 collective-permute-done.129
  659.8 7.4 collective-permute-done.130
  677.4 7.4 collective-permute-done.132
  693.3 7.8 collective-permute-done.134
  747.2 7.1 collective-permute-done.143
  786.0 11.0 fusion.549
  839.4 14.5 %collective-permute-done.157 = bf16[128,1664]{1,0:T(8,128)(2,1)S(1)} collective-permute-done((bf16[128,1664]{1,0:T(8,128)(2,1)S(1)}, bf16[128,1664]{1,0:T(8,128)(2,1)S(1)}, u32[]{:S(2)}, u32[]{:S(2)}) %collective-permute-start.157) | collective-permute-done | bytes 426016 | tf_op jit(solution)/shard_map/ppermute | solution.py:149
  858.0 8.2 collective-permute-done.158
  869.6 7.6 collective-permute-done.159
  906.9 8.7 copy.655
  932.4 9.3 collective-permute-done.209
  947.4 7.3 multiply_reduce_fusion.5
  985.0 7.2 collective-permute-done.169
  1088.4 8.1 collective-permute-done.175
  1207.1 7.8 fusion.1
  1218.2 9.6 collective-permute-done.191
  (1766 shorter events, 925.6 us)
Async XLA Ops:
  9.3 47.5 %collective-permute-start.1 = (bf16[96,1792]{1,0:T(8,128)(2,1)S(1)}, bf16[96,1792]{1,0:T(8,128)(2,1)}, u32[]{:S(2)}, u32[]{:S(2)}) collective-permute-start(bf16[96,1792]{1,0:T(8,128)(2,1)S(1)} %concatenate.346), channel_id=1, source_target_pairs={{0,8},{1,9},{2,10},{3,11},{4,12},{5,13},{6,14},{7,15},{8,16},{9,17... | collective-permute-start | bytes 1032200 | tf_op jit(solution)/shard_map/ppermute | solution.py:149
  12.4 44.5 %collective-permute-start.2 = (bf16[96,1792]{1,0:T(8,128)(2,1)S(1)}, bf16[96,1792]{1,0:T(8,128)(2,1)}, u32[]{:S(2)}, u32[]{:S(2)}) collective-permute-start(bf16[96,1792]{1,0:T(8,128)(2,1)S(1)} %concatenate.346), channel_id=1, source_target_pairs={{0,4},{1,5},{2,6},{3,7},{4,0},{5,1},{6,2},{7,3},{8,12},{9,13},{10,... | collective-permute-start | bytes 1032200 | tf_op jit(solution)/shard_map/ppermute | solution.py:149
  13.9 44.1 %collective-permute-start.110 = (bf16[128,1536]{1,0:T(8,128)(2,1)}, bf16[128,1536]{1,0:T(8,128)(2,1)S(1)}, u32[]{:S(2)}, u32[]{:S(2)}) collective-permute-start(bf16[128,1536]{1,0:T(8,128)(2,1)} %param.40), channel_id=1, source_target_pairs={{0,8},{1,9},{2,10},{3,11},{4,12},{5,13},{6,14},{7,15},{8,16},{9,17... | collective-permute-start | bytes 1179656 | tf_op jit(solution)/shard_map/ppermute | solution.py:149
  15.5 43.0 %collective-permute-start.111 = (bf16[128,1536]{1,0:T(8,128)(2,1)}, bf16[128,1536]{1,0:T(8,128)(2,1)S(1)}, u32[]{:S(2)}, u32[]{:S(2)}) collective-permute-start(bf16[128,1536]{1,0:T(8,128)(2,1)} %param.40), channel_id=1, source_target_pairs={{0,4},{1,5},{2,6},{3,7},{4,0},{5,1},{6,2},{7,3},{8,12},{9,13},{10,... | collective-permute-start | bytes 1179656 | tf_op jit(solution)/shard_map/ppermute | solution.py:149
  18.3 41.0 %collective-permute-start = (bf16[128,1536]{1,0:T(8,128)(2,1)S(1)}, bf16[128,1536]{1,0:T(8,128)(2,1)S(1)}, u32[]{:S(2)}, u32[]{:S(2)}) collective-permute-start(bf16[128,1536]{1,0:T(8,128)(2,1)S(1)} %fusion.281), channel_id=1, source_target_pairs={{0,1},{1,0},{2,3},{3,2},{4,5},{5,4},{6,7},{7,6},{8,9},{9,8},{10,11... | collective-permute-start | bytes 1179656 | tf_op jit(solution)/shard_map/ppermute | solution.py:149
  58.0 52.1 %collective-permute-start.8 = (bf16[96,1792]{1,0:T(8,128)(2,1)S(1)}, bf16[96,1792]{1,0:T(8,128)(2,1)S(1)}, u32[]{:S(2)}, u32[]{:S(2)}) collective-permute-start(bf16[96,1792]{1,0:T(8,128)(2,1)S(1)} %concatenate.346), channel_id=1, source_target_pairs={{0,2},{1,3},{2,0},{3,1},{4,6},{5,7},{6,4},{7,5},{8,10},{9,11},{10,... | collective-permute-start | bytes 1032200 | tf_op jit(solution)/shard_map/ppermute | solution.py:149
  97.4 195.7 %collective-permute-start.53 = (bf16[1536,256]{1,0:T(8,128)(2,1)}, bf16[1536,256]{1,0:T(8,128)(2,1)}, u32[]{:S(2)}, u32[]{:S(2)}) collective-permute-start(bf16[1536,256]{1,0:T(8,128)(2,1)} %bitcast.17), channel_id=1, source_target_pairs={{0,1},{1,0},{2,3},{3,2},{4,5},{5,4},{6,7},{7,6},{8,9},{9,8},{10,11... | collective-permute-start | bytes 2359304 | tf_op jit(solution)/shard_map/ppermute | solution.py:149
  97.9 195.1 %collective-permute-start.54 = (bf16[1536,256]{1,0:T(8,128)(2,1)}, bf16[1536,256]{1,0:T(8,128)(2,1)}, u32[]{:S(2)}, u32[]{:S(2)}) collective-permute-start(bf16[1536,256]{1,0:T(8,128)(2,1)} %bitcast.18), channel_id=1, source_target_pairs={{0,1},{1,0},{2,3},{3,2},{4,5},{5,4},{6,7},{7,6},{8,9},{9,8},{10,11... | collective-permute-start | bytes 2359304 | tf_op jit(solution)/shard_map/ppermute | solution.py:149
  125.4 92.9 %collective-permute-start.127 = (bf16[128,1536]{1,0:T(8,128)(2,1)}, bf16[128,1536]{1,0:T(8,128)(2,1)}, u32[]{:S(2)}, u32[]{:S(2)}) collective-permute-start(bf16[128,1536]{1,0:T(8,128)(2,1)} %collective-permute-done.125), channel_id=1, source_target_pairs={{0,2},{1,3},{2,0},{3,1},{4,6},{5,7},{6,4},{7,5},{8,10},{9,11},{10,... | collective-permute-start | bytes 1179656 | tf_op jit(solution)/shard_map/ppermute | solution.py:149
  152.5 69.1 %all-to-all-start = ((bf16[16,96,192]{1,2,0:T(8,128)(2,1)}), bf16[16,96,192]{1,2,0:T(8,128)(2,1)}, u32[]{:S(2)}, u32[]{:S(2)}) async-start(bf16[16,96,192]{1,2,0:T(8,128)(2,1)} %bitcast.29), calls=%async_computation | async-start | bytes 1572864 | tf_op jit(solution)/shard_map/all_to_all | solution.py:409
  157.7 308.6 %all-gather.2.cloned.1.call-start = ((), (), s32[]{:S(2)}) async-start(), calls=%async_computation.2 | async-start | bytes 6684672 | tf_op jit(solution)/shard_map/all_gather | solution.py:563
  224.2 127.6 %collective-permute-start.56 = (bf16[256,1536]{1,0:T(8,128)(2,1)}, bf16[256,1536]{1,0:T(8,128)(2,1)}, u32[]{:S(2)}, u32[]{:S(2)}) collective-permute-start(bf16[256,1536]{1,0:T(8,128)(2,1)} %bitcast.19), channel_id=1, source_target_pairs={{0,1},{1,0},{2,3},{3,2},{4,5},{5,4},{6,7},{7,6},{8,9},{9,8},{10,11... | collective-permute-start | bytes 2359304 | tf_op jit(solution)/shard_map/ppermute | solution.py:149
  407.1 84.4 %collective-permute-start.85 = (bf16[1536,256]{1,0:T(8,128)(2,1)}, bf16[1536,256]{1,0:T(8,128)(2,1)}, u32[]{:S(2)}, u32[]{:S(2)}) collective-permute-start(bf16[1536,256]{1,0:T(8,128)(2,1)} %bitcast.56), channel_id=1, source_target_pairs={{0,1},{1,0},{2,3},{3,2},{4,5},{5,4},{6,7},{7,6},{8,9},{9,8},{10,11... | collective-permute-start | bytes 2359304 | tf_op jit(solution)/shard_map/ppermute | solution.py:149
  408.7 82.9 %collective-permute-start.86 = (bf16[1536,256]{1,0:T(8,128)(2,1)}, bf16[1536,256]{1,0:T(8,128)(2,1)}, u32[]{:S(2)}, u32[]{:S(2)}) collective-permute-start(bf16[1536,256]{1,0:T(8,128)(2,1)} %bitcast.57), channel_id=1, source_target_pairs={{0,1},{1,0},{2,3},{3,2},{4,5},{5,4},{6,7},{7,6},{8,9},{9,8},{10,11... | collective-permute-start | bytes 2359304 | tf_op jit(solution)/shard_map/ppermute | solution.py:149
  409.2 52.3 %collective-permute-start.87 = (bf16[256,1536]{1,0:T(8,128)(2,1)}, bf16[256,1536]{1,0:T(8,128)(2,1)}, u32[]{:S(2)}, u32[]{:S(2)}) collective-permute-start(bf16[256,1536]{1,0:T(8,128)(2,1)} %bitcast.58), channel_id=1, source_target_pairs={{0,1},{1,0},{2,3},{3,2},{4,5},{5,4},{6,7},{7,6},{8,9},{9,8},{10,11... | collective-permute-start | bytes 2359304 | tf_op jit(solution)/shard_map/ppermute | solution.py:149
  421.4 44.1 %collective-permute-start.79 = (bf16[128,1536]{1,0:T(8,128)(2,1)S(1)}, bf16[128,1536]{1,0:T(8,128)(2,1)S(1)}, u32[]{:S(2)}, u32[]{:S(2)}) collective-permute-start(bf16[128,1536]{1,0:T(8,128)(2,1)S(1)} %multiply_convert_fusion.27), channel_id=1, source_target_pairs={{0,1},{1,0},{2,3},{3,2},{4,5},{5,4},{6,7},{7,6},{8,9},{9,8},{10,11... | collective-permute-start | bytes 1179656 | tf_op jit(solution)/shard_map/ppermute | solution.py:149
  576.3 49.4 %collective-permute-start.102 = (bf16[256,1536]{1,0:T(8,128)(2,1)S(1)}, bf16[256,1536]{1,0:T(8,128)(2,1)S(1)}, u32[]{:S(2)}, u32[]{:S(2)}) collective-permute-start(bf16[256,1536]{1,0:T(8,128)(2,1)S(1)} %slice.978), channel_id=1, source_target_pairs={{0,2},{1,3},{2,0},{3,1},{4,6},{5,7},{6,4},{7,5},{8,10},{9,11},{10,... | collective-permute-start | bytes 2359304 | tf_op jit(solution)/shard_map/ppermute | solution.py:149
  579.4 46.9 %collective-permute-start.98 = (bf16[256,1536]{1,0:T(8,128)(2,1)S(1)}, bf16[256,1536]{1,0:T(8,128)(2,1)S(1)}, u32[]{:S(2)}, u32[]{:S(2)}) collective-permute-start(bf16[256,1536]{1,0:T(8,128)(2,1)S(1)} %slice.975), channel_id=1, source_target_pairs={{0,2},{1,3},{2,0},{3,1},{4,6},{5,7},{6,4},{7,5},{8,10},{9,11},{10,... | collective-permute-start | bytes 2359304 | tf_op jit(solution)/shard_map/ppermute | solution.py:149
  579.8 43.1 %collective-permute-start.205 = (bf16[1536,256]{0,1:T(8,128)(2,1)}, bf16[1536,256]{0,1:T(8,128)(2,1)S(1)}, u32[]{:S(2)}, u32[]{:S(2)}) collective-permute-start(bf16[1536,256]{0,1:T(8,128)(2,1)} %get-tuple-element.741), channel_id=1, source_target_pairs={{0,1},{1,0},{2,3},{3,2},{4,5},{5,4},{6,7},{7,6},{8,9},{9,8},{10,11... | collective-permute-start | bytes 2359304 | tf_op jit(solution)/shard_map/ppermute | solution.py:149
  580.4 43.1 %collective-permute-start.206 = (bf16[1536,256]{0,1:T(8,128)(2,1)S(1)}, bf16[1536,256]{0,1:T(8,128)(2,1)S(1)}, u32[]{:S(2)}, u32[]{:S(2)}) collective-permute-start(bf16[1536,256]{0,1:T(8,128)(2,1)S(1)} %get-tuple-element.740), channel_id=1, source_target_pairs={{0,1},{1,0},{2,3},{3,2},{4,5},{5,4},{6,7},{7,6},{8,9},{9,8},{10,11... | collective-permute-start | bytes 2359304 | tf_op jit(solution)/shard_map/ppermute | solution.py:149
  581.8 40.9 %collective-permute-start.201 = (bf16[1536,96]{0,1:T(8,128)(2,1)S(1)}, bf16[1536,96]{0,1:T(8,128)(2,1)S(1)}, u32[]{:S(2)}, u32[]{:S(2)}) collective-permute-start(bf16[1536,96]{0,1:T(8,128)(2,1)S(1)} %pad_maximum_fusion.35), channel_id=1, source_target_pairs={{0,1},{1,0},{2,3},{3,2},{4,5},{5,4},{6,7},{7,6},{8,9},{9,8},{10,11... | collective-permute-start | bytes 884744 | tf_op jit(solution)/shard_map/ppermute | solution.py:149
  627.4 78.0 %collective-permute-start.207 = (bf16[256,1536]{1,0:T(8,128)(2,1)S(1)}, bf16[256,1536]{1,0:T(8,128)(2,1)S(1)}, u32[]{:S(2)}, u32[]{:S(2)}) collective-permute-start(bf16[256,1536]{1,0:T(8,128)(2,1)S(1)} %slice.1440), channel_id=1, source_target_pairs={{0,1},{1,0},{2,3},{3,2},{4,5},{5,4},{6,7},{7,6},{8,9},{9,8},{10,11... | collective-permute-start | bytes 2359304 | tf_op jit(solution)/shard_map/ppermute | solution.py:149
  801.4 34.7 %collective-permute-start.152 = (bf16[256,1664]{1,0:T(8,128)(2,1)}, bf16[256,1664]{1,0:T(8,128)(2,1)}, u32[]{:S(2)}, u32[]{:S(2)}) collective-permute-start(bf16[256,1664]{1,0:T(8,128)(2,1)} %pad_maximum_fusion.12), channel_id=1, source_target_pairs={{0,2},{1,3},{2,0},{3,1},{4,6},{5,7},{6,4},{7,5},{8,10},{9,11},{10,... | collective-permute-start | bytes 2555912 | tf_op jit(solution)/shard_map/ppermute | solution.py:149
  802.8 52.3 %collective-permute-start.147 = (bf16[256,1664]{1,0:T(8,128)(2,1)}, bf16[256,1664]{1,0:T(8,128)(2,1)}, u32[]{:S(2)}, u32[]{:S(2)}) collective-permute-start(bf16[256,1664]{1,0:T(8,128)(2,1)} %pad_maximum_fusion.13), channel_id=1, source_target_pairs={{0,2},{1,3},{2,0},{3,1},{4,6},{5,7},{6,4},{7,5},{8,10},{9,11},{10,... | collective-permute-start | bytes 2555912 | tf_op jit(solution)/shard_map/ppermute | solution.py:149
  803.9 73.9 %collective-permute-start.142 = (bf16[256,1664]{1,0:T(8,128)(2,1)}, bf16[256,1664]{1,0:T(8,128)(2,1)}, u32[]{:S(2)}, u32[]{:S(2)}) collective-permute-start(bf16[256,1664]{1,0:T(8,128)(2,1)} %pad_maximum_fusion.14), channel_id=1, source_target_pairs={{0,2},{1,3},{2,0},{3,1},{4,6},{5,7},{6,4},{7,5},{8,10},{9,11},{10,... | collective-permute-start | bytes 2555912 | tf_op jit(solution)/shard_map/ppermute | solution.py:149
  820.9 100.9 %collective-permute-start.204 = (bf16[256,1536]{1,0:T(8,128)(2,1)}, bf16[256,1536]{1,0:T(8,128)(2,1)}, u32[]{:S(2)}, u32[]{:S(2)}) collective-permute-start(bf16[256,1536]{1,0:T(8,128)(2,1)} %slice.1441), channel_id=1, source_target_pairs={{0,1},{1,0},{2,3},{3,2},{4,5},{5,4},{6,7},{7,6},{8,9},{9,8},{10,11... | collective-permute-start | bytes 2359304 | tf_op jit(solution)/shard_map/ppermute | solution.py:149
  827.7 103.3 %all-to-all-start.1 = ((bf16[16,96,192]{1,2,0:T(8,128)(2,1)}), bf16[16,96,192]{1,2,0:T(8,128)(2,1)}, u32[]{:S(2)}, u32[]{:S(2)}) async-start(bf16[16,96,192]{1,2,0:T(8,128)(2,1)} %copy.674), calls=%async_computation.1 | async-start | bytes 1572864 | tf_op jit(solution)/shard_map/all_to_all | solution.py:671
  833.3 58.5 %collective-permute-start.202 = (bf16[1536,256]{0,1:T(8,128)(2,1)}, bf16[1536,256]{0,1:T(8,128)(2,1)S(1)}, u32[]{:S(2)}, u32[]{:S(2)}) collective-permute-start(bf16[1536,256]{0,1:T(8,128)(2,1)} %get-tuple-element.743), channel_id=1, source_target_pairs={{0,1},{1,0},{2,3},{3,2},{4,5},{5,4},{6,7},{7,6},{8,9},{9,8},{10,11... | collective-permute-start | bytes 2359304 | tf_op jit(solution)/shard_map/ppermute | solution.py:149
  853.9 37.9 %collective-permute-start.203 = (bf16[1536,256]{0,1:T(8,128)(2,1)S(1)}, bf16[1536,256]{0,1:T(8,128)(2,1)S(1)}, u32[]{:S(2)}, u32[]{:S(2)}) collective-permute-start(bf16[1536,256]{0,1:T(8,128)(2,1)S(1)} %copy-done.109), channel_id=1, source_target_pairs={{0,1},{1,0},{2,3},{3,2},{4,5},{5,4},{6,7},{7,6},{8,9},{9,8},{10,11... | collective-permute-start | bytes 2359304 | tf_op jit(solution)/shard_map/ppermute | solution.py:149
  919.6 42.9 %collective-permute-start.166 = (bf16[8,96,2048]{2,1,0:T(8,128)(2,1)}, bf16[8,96,2048]{2,1,0:T(8,128)(2,1)}, u32[]{:S(2)}, u32[]{:S(2)}) collective-permute-start(bf16[8,96,2048]{2,1,0:T(8,128)(2,1)} %dynamic-slice_bitcast_fusion), channel_id=1, source_target_pairs={{0,2},{1,3},{2,0},{3,1},{4,6},{5,7},{6,4},{7,5},{8,10},{9,11},{10,... | collective-permute-start | bytes 9437192 | tf_op jit(solution)/shard_map/ppermute | solution.py:149
  1045.2 38.7 %collective-permute-start.174 = (bf16[8,96,1536]{2,1,0:T(8,128)(2,1)}, bf16[8,96,1536]{2,1,0:T(8,128)(2,1)}, u32[]{:S(2)}, u32[]{:S(2)}) collective-permute-start(bf16[8,96,1536]{2,1,0:T(8,128)(2,1)} %dynamic-slice_bitcast_fusion.2), channel_id=1, source_target_pairs={{0,2},{1,3},{2,0},{3,1},{4,6},{5,7},{6,4},{7,5},{8,10},{9,11},{10,... | collective-permute-start | bytes 7077896 | tf_op jit(solution)/shard_map/ppermute | solution.py:149
  1063.1 81.7 %collective-permute-start.190 = (bf16[256,128]{1,0:T(8,128)(2,1)}, bf16[256,128]{1,0:T(8,128)(2,1)}, u32[]{:S(2)}, u32[]{:S(2)}) collective-permute-start(bf16[256,128]{1,0:T(8,128)(2,1)} %bitcast.131), channel_id=1, source_target_pairs={{0,1},{1,0},{2,3},{3,2},{4,5},{5,4},{6,7},{7,6},{8,9},{9,8},{10,11... | collective-permute-start | bytes 196616 | tf_op jit(solution)/shard_map/ppermute | solution.py:149
  (535 other events, 6367.1 us)
Sparse Core Ops, SparseCore 0:
  301.5 70.5 all-gather.1

commit v2 on v1

v2 whole, which is shorter than its diff:
```python
import jax
import jax.numpy as jnp
from jax import lax
from jax.sharding import PartitionSpec as P

MH = 48
NS = 128
CH = 128
QUERY_HEADS = 12
KEY_VALUE_HEADS = 4
HEAD_SIZE = 128
TOP = 6
LEN = 256
DI = 3072


EPS = 1e-05
HIGH = lax.Precision.HIGHEST


def matmul(left, right):
    return jnp.dot(left, right, preferred_element_type=jnp.float32)


def times_back(left, right):
    return lax.dot_general(
        left, right, (((1,), (1,)), ((), ())), preferred_element_type=jnp.float32
    )


def times_over(left, right):
    return lax.dot_general(
        left, right, (((0,), (0,)), ((), ())), preferred_element_type=jnp.float32
    )


def rms_norm(value_rows, gain):
    return value_rows * lax.rsqrt(jnp.mean(value_rows * value_rows, -1, keepdims=True) + EPS) * gain


def causal_conv(value_rows, weight, bias):
    width = weight.shape[0]
    sequence_length = value_rows.shape[0]
    padded = jnp.concatenate(
        [jnp.zeros((width - 1, value_rows.shape[1]), jnp.float32), value_rows], 0
    )
    total = jnp.zeros_like(value_rows) + bias[None, :]
    for shift in range(width):
        total = total + weight[shift][None, :] * padded[shift : shift + sequence_length]
    return total


def conv_act(value_rows, weight, bias):
    return jax.nn.silu(causal_conv(value_rows, weight, bias))


def silu_slope(value_rows):
    sig = jax.nn.sigmoid(value_rows)
    return sig * (1.0 + value_rows * (1.0 - sig))


AXES = ("dp", "tensor")
SPARE = 128
MASK_COLUMNS = 384
SCAN = lax.Precision.DEFAULT
MOST_ROWS = 4096


def scan_block(x_blk, step_blk, step_bias, decay_log, skip_gain, b_blk, c_blk, state, more):
    rows = x_blk.shape[0]
    lower = (jnp.arange(rows)[:, None] >= jnp.arange(rows)[None, :])[:, :, None]
    d_blk = jax.nn.softplus(step_blk + step_bias[None, :])
    cum = jnp.cumsum(d_blk * -jnp.exp(decay_log)[None, :], 0)
    diff = jnp.where(lower, cum[:, None, :] - cum[None, :, :], 0.0)
    decay = jnp.where(lower, jnp.exp(diff), 0.0)
    inner = jnp.dot(c_blk, b_blk.T, precision=SCAN)
    weights = inner[:, :, None] * decay * d_blk[None, :, :]
    out = jnp.einsum("ijh,jhp->ihp", weights, x_blk, precision=SCAN) + skip_gain[None, :, None] * x_blk
    if state is not None:
        out = out + jnp.exp(cum)[:, :, None] * jnp.einsum(
            "in,hpn->ihp", c_blk, state, precision=SCAN
        )
    if not more:
        return None, out
    tail = jnp.exp(cum[-1][None, :] - cum) * d_blk
    update = jnp.einsum("jhp,jn->hpn", tail[:, :, None] * x_blk, b_blk, precision=SCAN)
    if state is not None:
        update = update + jnp.exp(cum[-1])[:, None, None] * state
    return update, out


def total_of(left, right):
    return left.astype(jnp.float32) + right.astype(jnp.float32)


def low(value_rows):
    return value_rows.astype(jnp.bfloat16)


def together(values):
    return lax.optimization_barrier(values)


def after(value, *others):
    return lax.optimization_barrier((value, others))[0]


class Beside:
    def __init__(self, work=None):
        self.work = work
        self.result = None
        self.pending = None
        if work is not None:
            self.advance(None)

    def advance(self, value):
        try:
            self.pending = self.work.send(value)
        except StopIteration as stop:
            self.work, self.result = None, stop.value

    def together(self, held):
        if self.work is None:
            return together(held)
        held, value = together((held, self.pending))
        self.advance(value)
        return held

    def finish(self):
        while self.work is not None:
            self.advance(self.pending)
        return self.result


class Grid:
    def __init__(self):
        self.dp = lax.axis_size("dp")
        self.nt = lax.axis_size("tensor")
        self.nc = 2
        self.na = 4
        self.nb = self.dp // (self.na * self.nc)
        index = lax.axis_index("dp")
        self.index = index
        self.c = index % self.nc
        self.b = (index // self.nc) % self.nb
        self.a = index // (self.nc * self.nb)
        self.t = lax.axis_index("tensor")
        self.step_t = (1, self.nt)
        self.step_c = (self.nt, self.nc)
        self.step_b = (self.nt * self.nc, self.nb)
        self.step_a = (self.nt * self.nc * self.nb, self.na)

    def shift(self, value, step, amount):
        stride, size = step
        pairs = []
        for source in range(self.dp * self.nt):
            digit = (source // stride) % size
            pairs.append((source, source + ((digit + amount) % size - digit) * stride))
        return lax.ppermute(value, AXES, pairs)

    def around(self, value, step):
        held = [value]
        for _ in range(step[1] - 1):
            held.append(self.shift(held[-1], step, 1))
        return held

    def sum_around(self, part, step):
        size = step[1]
        held = part(size - 1)
        for k in range(size - 2, -1, -1):
            held = total_of(part(k), self.shift(low(held), step, -1))
        return held

    def rounds(self, value, beside=None):
        beside = beside or Beside()
        for k in range(self.na):
            ahead = self.shift(value, self.step_a, 1) if k < self.na - 1 else value
            near = self.around(value, self.step_b)
            ahead, near = beside.together((ahead, near))
            yield near
            value = ahead

    def nearby(self):
        return [
            [
                (((self.a - k) % self.na) * self.nb + (self.b - kb) % self.nb) * self.nc
                + (self.c - kc) % self.nc
                for kc in range(self.nc)
                for kb in range(self.nb)
            ]
            for k in range(self.na)
        ]

    def with_core(self, near):
        half = jnp.concatenate(near, 0)
        return jnp.concatenate([half, self.shift(half, self.step_c, 1)], 0)

    def core_sum(self, value):
        half = value.shape[0] // 2
        return low(total_of(value[:half], self.shift(value[half:], self.step_c, 1)))

    def collect_rounds(self, parts, beside=None):
        beside = beside or Beside()
        total = None
        for k in range(self.na - 1, -1, -1):
            part = parts[k]
            count = part.shape[0] // self.nb
            moved = None
            if total is not None:
                part, total = together((part, low(total)))
                moved = self.shift(total, self.step_a, -1)
            near = self.sum_around(lambda kb: part[kb * count : (kb + 1) * count], self.step_b)
            near, moved = beside.together((near, moved))
            total = near if moved is None else total_of(near, moved)
        return total

    def core_product(self, left, right):
        half = left.shape[1] // 2
        got = self.shift(low(times_over(left[:, half:], right)), self.step_c, 1)
        return low(total_of(times_over(left[:, :half], right), got))

    def scatter_ordered(self, value, beside=None):
        count = value.shape[0] // self.na
        return self.collect_rounds(
            [value[k * count : (k + 1) * count] for k in range(self.na)], beside
        )

    def long(self, value):
        return self.dp * value.shape[0] > MOST_ROWS

    def turn(self, step, value, rest, ready=None, reduce=None):
        if self.long(value):

            def advance(carry, item):
                held, total = carry
                every, item = item
                if every is None:
                    every = self.with_core(self.around(held, self.step_b))
                    held = self.shift(held, self.step_a, 1)
                part, *others = step(every, item)
                if reduce is not None:
                    total = [old + new for old, new in zip(total, reduce(item, others))]
                    others = []
                return (held, total), (part, others)

            total = []
            if reduce is not None:
                item = tuple(leaf[0] for leaf in rest)
                every = jax.ShapeDtypeStruct((rest[0].shape[1], value.shape[1]), value.dtype)
                shapes = jax.eval_shape(lambda *args: reduce(args[1], step(*args)[1:]), every, item)
                total = [jnp.zeros(shape.shape, jnp.float32) for shape in shapes]
            ready = None if ready is None else jnp.stack(ready)
            (_, total), (parts, others) = lax.scan(advance, (value, total), (ready, rest))
            return parts, (others if reduce is None else total)
        items = [tuple(leaf[k] for leaf in rest) for k in range(self.na)]
        if ready is not None:
            results = [step(*pair) for pair in zip(ready, items)]
        else:
            results = []
            for k in range(self.na):
                ahead = self.shift(value, self.step_a, 1) if k < self.na - 1 else value
                near = self.around(value, self.step_b)
                ahead, near = together((ahead, near))
                results.append(step(self.with_core(near), items[k]))
                value = ahead
        parts, *others = [list(leaves) for leaves in zip(*results)]
        return parts, others

    def gather_weight(self, value, beside=None):
        held = []
        for near in self.rounds(value, beside):
            held.extend(near)
        return self.with_core(held)

    def order(self, rows):
        at = jnp.arange(self.dp * rows, dtype=jnp.int32)
        kc, ka, kb = (
            at // (rows * self.nb * self.na),
            (at // (rows * self.nb)) % self.na,
            (at // rows) % self.nb,
        )
        a, b, c = (self.a - ka) % self.na, (self.b - kb) % self.nb, (self.c - kc) % self.nc
        source = ((a * self.nb + b) * self.nc + c) * rows + at % rows
        return low(jnp.arange(self.dp * rows, dtype=jnp.int32)[:, None] == source[None, :])

    def all_sum(self, value):
        half = value.shape[0] // 2
        keep = lax.dynamic_slice_in_dim(value, self.c * half, half, 0)
        send = lax.dynamic_slice_in_dim(value, (1 - self.c) * half, half, 0)
        yield ()
        value = keep + self.shift(send, self.step_c, 1)
        value = yield sum(self.around(value, self.step_t))
        value = yield sum(self.around(value, self.step_b))
        value = yield value + sum(self.shift(value, self.step_a, k) for k in range(1, self.na))
        other = self.shift(value, self.step_c, 1)
        return jnp.where(
            self.c == 0,
            jnp.concatenate([value, other], 0),
            jnp.concatenate([other, value], 0),
        )

    def swap(self, value):
        return self.shift(value, self.step_t, 1)

    def swap_in_turn(self, values):
        found = []
        for value in values:
            found.append(self.swap(after(value, found[-1]) if found else value))
        return found

    def pair_rows(self, value):
        other = self.swap(value)
        return jnp.where(
            self.t == 0,
            jnp.concatenate([value, other], 0),
            jnp.concatenate([other, value], 0),
        )

    def pair_sum(self, value, axis):
        half = value.shape[axis] // 2
        keep = lax.dynamic_slice_in_dim(value, self.t * half, half, axis)
        send = lax.dynamic_slice_in_dim(value, (1 - self.t) * half, half, axis)
        return total_of(keep, self.swap(low(send)))


def dense_gates(logits, picked):
    shown = jnp.where(picked, logits, -1e30)
    raised = jnp.where(picked, jnp.exp(logits - jnp.max(shown, 1, keepdims=True)), 0.0)
    return raised / jnp.sum(raised, 1, keepdims=True)


def body(
    hidden_in,
    out_grad,
    routes_first,
    routes_second,
    in_gate,
    in_value,
    in_state,
    in_step,
    mix_output,
    attn_query,
    attention_key_matrix,
    attention_value_matrix,
    attn_output,
    shared_gate_one,
    shared_up_one,
    shared_down_one,
    shared_gate_two,
    shared_up_two,
    shared_down_two,
    expert_gate_one,
    expert_up_one,
    expert_down_one,
    expert_gate_two,
    expert_up_two,
    expert_down_two,
    router_one,
    router_two,
    norm_mix,
    norm_moe_one,
    norm_attn,
    norm_moe_two,
    gated_norm,
    conv_value_weight,
    conv_value_bias,
    conv_state_weight,
    conv_state_bias,
    step_bias,
    decay_log,
    skip_gain,
):
    grid = Grid()
    tensor_rank = grid.t
    expert_count = grid.dp
    local_rows = hidden_in.shape[0]
    value_cols = in_value.shape[1]
    state_cols = in_state.shape[1]
    head_cols = in_step.shape[1]
    value_start = tensor_rank * value_cols
    state_start = tensor_rank * state_cols
    head_start = tensor_rank * head_cols
    norm_local = lax.dynamic_slice_in_dim(gated_norm, value_start, value_cols, 0)
    value_kernel = lax.dynamic_slice_in_dim(conv_value_weight, value_start, value_cols, 1)
    value_offset = lax.dynamic_slice_in_dim(conv_value_bias, value_start, value_cols, 0)
    state_kernel = lax.dynamic_slice_in_dim(conv_state_weight, state_start, state_cols, 1)
    state_offset = lax.dynamic_slice_in_dim(conv_state_bias, state_start, state_cols, 0)
    bias_local = lax.dynamic_slice_in_dim(step_bias, head_start, head_cols, 0)
    decay_local = lax.dynamic_slice_in_dim(decay_log, head_start, head_cols, 0)
    skip_local = lax.dynamic_slice_in_dim(skip_gain, head_start, head_cols, 0)
    scale = HEAD_SIZE ** (-0.5)
    model = hidden_in.shape[1]
    narrow = state_cols + head_cols
    block_rows = in_value.shape[0]

    rows = hidden_in.astype(jnp.float32)
    normalized_input, norm_pull = jax.vjp(rms_norm, rows, norm_mix)
    full = grid.pair_rows(low(normalized_input))
    sequence_length = full.shape[0]
    order = grid.order(block_rows)

    w_first = grid.gather_weight(
        jnp.concatenate(
            [in_value, in_state, in_step, jnp.zeros((block_rows, -narrow % 128), jnp.bfloat16)], 1
        )
    )
    value_weight = w_first[:, :value_cols]
    w_narrow = w_first[:, value_cols:]
    w_out_t = lax.all_gather(mix_output.T, "dp", axis=0, tiled=True)
    w_attention = lax.all_gather(
        after(
            jnp.concatenate(
                [attn_query, attention_key_matrix, attention_value_matrix, attn_output.T], 1
            ),
            w_out_t,
        ),
        "dp",
        axis=0,
        tiled=True,
    )
    q_cols = attn_query.shape[1]
    k_cols = attention_key_matrix.shape[1]
    wide_cols = q_cols + 2 * k_cols

    shared_units = shared_gate_one.shape[1] // expert_count
    shared_parts = jnp.stack(
        [
            shared_gate_one,
            shared_up_one,
            shared_down_one.T,
            shared_gate_two,
            shared_up_two,
            shared_down_two.T,
        ],
        1,
    ).reshape(block_rows, 6, expert_count, shared_units)
    shared_parts = shared_parts.transpose(2, 0, 1, 3)
    shared_own = lax.all_to_all(
        after(shared_parts.reshape(expert_count, block_rows, 6 * shared_units), w_first),
        "dp",
        split_axis=0,
        concat_axis=0,
        tiled=True,
    ).reshape(model, 6 * shared_units)
    shared_other = grid.swap(shared_own)

    def shared_of(which):
        at = which * shared_units
        return [
            shared_own[:, at : at + shared_units],
            shared_other[:, at : at + shared_units],
        ]

    def expert_weights(bank, which, when):
        own = [leaf[0] for leaf in bank]
        gate_other, up_other, down_other = grid.swap_in_turn(after(own, when))
        gate_own, up_own, down_own = own
        narrow_in = together(jnp.concatenate(shared_of(which) + shared_of(which + 1), 1))
        w_in = jnp.concatenate([gate_own, gate_other, up_own, up_other, narrow_in], 1)
        down_t = jnp.concatenate(shared_of(which + 2), 1)
        w_down = jnp.concatenate([down_own, down_other, down_t.T], 0)
        return w_in, w_down

    experts_one = expert_weights((expert_gate_one, expert_up_one, expert_down_one), 0, full)
    half_units = expert_gate_one.shape[2]
    units = 2 * half_units
    pair_units = 2 * shared_units

    def local_mask(routes):
        mine = lax.dynamic_slice_in_dim(routes, tensor_rank * local_rows, local_rows, 0)
        names = jnp.arange(expert_count, dtype=jnp.int32)
        return jnp.any(mine[:, :, None] == names[None, None, :], 1)

    mask_one, mask_two = local_mask(routes_first), local_mask(routes_second)
    masks = low(jnp.concatenate([mask_one, mask_two], 1))
    spare_columns = max(0, MASK_COLUMNS - masks.shape[1])
    masks = lax.all_gather(jnp.pad(masks, ((0, 0), (0, spare_columns))), "dp", axis=0)
    masks = [
        jnp.concatenate([masks[at, :, : 2 * expert_count] for at in blocks], 0) > 0.5
        for blocks in grid.nearby()
    ]
    picked_one = jnp.stack([mask[:, :expert_count] for mask in masks])
    picked_two = jnp.stack([mask[:, expert_count:] for mask in masks])
    here = (jnp.arange(expert_count, dtype=jnp.int32) == grid.index)[None, :]

    def split_up(before):
        wide = before.astype(jnp.float32)
        edges = [units, 2 * units, 2 * units + pair_units]
        return jnp.split(wide, edges, 1)

    def moe_forward(rows, gain, router, picked, weights):
        w_in, w_down = weights
        normalized_input, norm_pull = jax.vjp(rms_norm, rows, gain)
        local = low(normalized_input)

        def step(every, chunk):
            (chosen,) = chunk
            gates = dense_gates(matmul(every, router), chosen)
            gate = jnp.sum(jnp.where(here, gates, 0.0), 1, keepdims=True)
            before = low(matmul(every, w_in))
            first, second, shared_a, shared_b = split_up(before)
            hidden = jnp.concatenate(
                [
                    low(jax.nn.silu(first) * second * gate),
                    low(jax.nn.silu(shared_a) * shared_b),
                ],
                1,
            )
            part = grid.core_sum(low(matmul(hidden, w_down)))
            return (part, every, gate, before, hidden)

        parts, kept = grid.turn(step, local, (picked,))
        return parts, (norm_pull, local, kept)

    def moe_backward(grad, router, local_picked, weights, keep, ready=None):
        w_in, w_down = weights
        norm_pull, local, kept = keep
        spare = jnp.arange(SPARE, dtype=jnp.int32)[None, :] == grid.index

        def step(d_every, chunk):
            _, gate, before, _ = chunk
            first, second, shared_a, shared_b = split_up(before)
            d_before = low(times_back(d_every, w_down)).astype(jnp.float32)
            d_hidden, d_shared = d_before[:, :units], d_before[:, units:]
            active = jax.nn.silu(first)
            d_gate = jnp.sum(d_hidden * active * second, 1, keepdims=True)
            d_hidden = d_hidden * gate
            d_in = jnp.concatenate(
                [
                    low(d_hidden * second * silu_slope(first)),
                    low(d_hidden * active),
                    low(d_shared * shared_b * silu_slope(shared_a)),
                    low(d_shared * jax.nn.silu(shared_a)),
                ],
                1,
            )
            d_in = together(d_in)
            sent = jnp.concatenate(
                [low(times_back(d_in, w_in)), low(jnp.where(spare, d_gate, 0.0))], 1
            )
            return (grid.core_sum(sent), d_every, d_in)

        def reduce(chunk, more):
            every, _, _, hidden = chunk
            d_every, d_in = more
            return times_over(every, d_in), times_over(hidden, d_every)

        parts, others = grid.turn(step, low(grad), kept, ready, reduce)
        if grid.long(grad):
            got = grid.collect_rounds(parts)
            g_in, g_down = others
        else:
            got = grid.collect_rounds(parts)
        others = others if grid.long(grad) else (kept[0], kept[3], *others)
        gates = dense_gates(matmul(local, router), local_picked)
        d_gates = got[:, model : model + expert_count]
        d_logits = low(gates * (d_gates - jnp.sum(gates * d_gates, 1, keepdims=True)))
        d_local = got[:, :model] + times_back(d_logits, router)
        g_router = times_over(d_logits, local)
        d_rows, g_gain = norm_pull(d_local)
        return (grad + d_rows, g_gain, g_router, others)

    def expert_grads(others, when):
        if len(others) == 2:
            g_in, g_down = others
        else:
            every, hidden, d_every, d_in = [
                jnp.concatenate(list(leaf), 0) for leaf in after(others, when)
            ]
            g_in, g_down = times_over(every, d_in), times_over(hidden, d_every)
        own, other = slice(0, half_units), slice(half_units, units)
        own_up = slice(units, units + half_units)
        other_up = slice(units + half_units, 2 * units)
        g_rest, g_rest_down = g_in[:, 2 * units :], g_down[units:].T
        s = shared_units
        mine = jnp.concatenate([g_rest[:, :s], g_rest[:, 2 * s : 3 * s], g_rest_down[:, :s]], 1)
        theirs = jnp.concatenate([g_rest[:, s : 2 * s], g_rest[:, 3 * s :], g_rest_down[:, s:]], 1)
        theirs, g_gate_other, g_up_other, g_down_other = grid.swap_in_turn(
            (low(theirs), low(g_in[:, other]), low(g_in[:, other_up]), low(g_down[other]))
        )
        g_shared = low(mine + theirs)
        g_experts = (
            (g_in[:, own] + g_gate_other)[None],
            (g_in[:, own_up] + g_up_other)[None],
            (g_down[own] + g_down_other)[None],
        )
        return g_shared, g_experts

    def sum_weight(value):
        return lax.psum_scatter(value, "dp", scatter_dimension=0, tiled=True).astype(jnp.float32)

    heads = head_cols
    block_count = sequence_length // CH

    def cut(value):
        return [value[at * CH : (at + 1) * CH] for at in range(block_count)]

    def mixer_forward():
        ordered = low(matmul(full, order))
        value_pre = matmul(ordered, value_weight)
        narrow_pre = matmul(ordered, w_narrow)
        state_pre = narrow_pre[:, :state_cols]
        step_pre = narrow_pre[:, state_cols:narrow]
        value_act, value_pull = jax.vjp(conv_act, value_pre, value_kernel, value_offset)
        state_act, state_pull = jax.vjp(conv_act, state_pre, state_kernel, state_offset)
        state_own = low(state_act)
        state_other = grid.swap(state_own)
        value_act, state_own, state_other = yield (value_act, state_own, state_other)
        in_map = jnp.where(tensor_rank == 0, state_own, state_other).astype(jnp.float32)
        out_map = jnp.where(tensor_rank == 0, state_other, state_own).astype(jnp.float32)
        state, outs, pulls = None, [], []
        cuts = zip(cut(value_act.reshape(sequence_length, heads, -1)), cut(step_pre), cut(in_map), cut(out_map))
        for at, (x_blk, step_blk, b_blk, c_blk) in enumerate(cuts):
            more = at < block_count - 1

            def block(x_blk, step_blk, bias, decay, skip, b_blk, c_blk, state, more=more):
                return scan_block(x_blk, step_blk, bias, decay, skip, b_blk, c_blk, state, more)

            (state, out), pull = jax.vjp(
                block, x_blk, step_blk, bias_local, decay_local, skip_local, b_blk, c_blk, state
            )
            state, out = yield (state, out)
            outs.append(out.reshape(CH, -1))
            pulls.append(pull)
        return ordered, jnp.concatenate(outs, 0), value_pull, state_pull, pulls

    work = Beside(mixer_forward())
    w_gate = grid.gather_weight(after(in_gate, w_first), work)
    ordered, ssm_out, value_pull, state_pull, scan_pulls = work.finish()

    gate_pre = matmul(ordered, w_gate)
    gated = ssm_out * jax.nn.silu(gate_pre)
    square = jnp.sum(gated * gated, 1, keepdims=True)
    inverse = lax.rsqrt((square + grid.swap(square)) / DI + EPS)
    mixed = low(gated * inverse * norm_local)
    mixed_out = times_back(mixed, w_out_t)
    result = rows + grid.pair_sum(mixed_out, 0)
    experts_two = expert_weights((expert_gate_two, expert_up_two, expert_down_two), 3, result)
    qkv_weight = w_attention[:, :wide_cols]
    attn_out_t = w_attention[:, wide_cols:]
    parts, moe_one_keep = moe_forward(result, norm_moe_one, router_one, picked_one, experts_one)
    parts, experts_two = together((parts, experts_two))
    state_two = result + grid.collect_rounds(parts)

    normalized_input, attention_norm_pull = jax.vjp(rms_norm, state_two, norm_attn)
    attention_full = grid.pair_rows(low(normalized_input))
    kv_heads = k_cols // HEAD_SIZE
    query_groups = QUERY_HEADS // KEY_VALUE_HEADS

    def attention_forward():
        qkv = low(matmul(attention_full, qkv_weight))
        query_rows = qkv[:, :q_cols].reshape(sequence_length, kv_heads, query_groups, HEAD_SIZE)
        key_rows = qkv[:, q_cols : q_cols + k_cols].reshape(sequence_length, kv_heads, HEAD_SIZE)
        value_rows = qkv[:, q_cols + k_cols :].reshape(sequence_length, kv_heads, HEAD_SIZE)
        causal = jnp.arange(sequence_length)[:, None] >= jnp.arange(sequence_length)[None, :]
        scores = (
            jnp.einsum("ikgd,jkd->kgij", query_rows, key_rows, preferred_element_type=jnp.float32)
            * scale
        )
        scores = jnp.where(causal, scores, -1e30)
        peak = jnp.max(scores, 3, keepdims=True)
        raised = jnp.exp(scores - peak)
        probs = yield raised / jnp.sum(raised, 3, keepdims=True)
        low_probs = low(probs)
        attended = jnp.einsum(
            "kgij,jkd->ikgd", low_probs, value_rows, preferred_element_type=jnp.float32
        )
        attended = low(attended.reshape(sequence_length, -1))
        output = yield grid.pair_sum(times_back(attended, attn_out_t), 0)
        return query_rows, key_rows, value_rows, probs, low_probs, attended, state_two + output

    work = Beside(attention_forward())
    d_every_two = [
        grid.with_core(near) for near in grid.rounds(after(out_grad, attention_full), work)
    ]
    query_rows, key_rows, value_rows, probs, low_probs, attended, result = work.finish()
    output_parts, moe_two_keep = moe_forward(
        result, norm_moe_two, router_two, picked_two, experts_two
    )
    forward_rows = result

    grad = out_grad.astype(jnp.float32)
    grad, g_nmoe_two, g_router_two, weights_two = moe_backward(
        grad, router_two, mask_two, experts_two, moe_two_keep, d_every_two
    )
    g_shared_two, g_experts_two = expert_grads(weights_two, grad)

    dfull = grid.pair_rows(low(grad))

    def attention_backward():
        d_att = low(matmul(dfull, attn_out_t)).reshape(query_rows.shape)
        d_probs = jnp.einsum(
            "ikgd,jkd->kgij", d_att, value_rows, preferred_element_type=jnp.float32
        )
        d_scores = low(probs * (d_probs - jnp.sum(probs * d_probs, 3, keepdims=True)))
        d_att, d_scores = yield (d_att, d_scores)
        d_query = low(
            jnp.einsum("kgij,jkd->ikgd", d_scores, key_rows, preferred_element_type=jnp.float32)
            * scale
        ).reshape(sequence_length, -1)
        d_keys = low(
            jnp.einsum("kgij,ikgd->jkd", d_scores, query_rows, preferred_element_type=jnp.float32)
            * scale
        ).reshape(sequence_length, -1)
        d_values = low(
            jnp.einsum("kgij,ikgd->jkd", low_probs, d_att, preferred_element_type=jnp.float32)
        ).reshape(sequence_length, -1)
        d_qkv = jnp.concatenate([d_query, d_keys, d_values], 1)
        d_qkv, d_normed = yield (d_qkv, grid.pair_sum(times_back(d_qkv, qkv_weight), 0))
        g_out_t = low(times_over(dfull, attended))
        g_qkv = low(times_over(attention_full, d_qkv))
        g_all = yield jnp.concatenate([g_qkv, g_out_t], 1)
        return d_normed, g_all

    work = Beside(attention_backward())
    output_parts, dfull = together((output_parts, dfull))
    block_out = forward_rows + grid.collect_rounds(output_parts, work)
    d_normed, g_attention = work.finish()
    attention_sum = sum_weight(g_attention)
    d_rows, g_nattn = attention_norm_pull(d_normed)
    grad = grad + d_rows

    grad, g_nmoe_one, g_router_one, weights_one = moe_backward(
        grad, router_one, mask_one, experts_one, moe_one_keep
    )

    dfull, g_experts_two = together((grid.pair_rows(low(grad)), g_experts_two))
    kept_gate = []

    def mixer_backward():
        d_mixed = matmul(dfull, w_out_t)
        weighted = d_mixed * norm_local
        total = jnp.sum(weighted * gated, 1, keepdims=True)
        total = total + grid.swap(total)
        d_gated = weighted * inverse - gated * inverse**3 * (total / DI)
        g_ngated = jnp.sum(d_mixed * gated * inverse, 0)
        d_ssm, low_gate = yield (
            d_gated * jax.nn.silu(gate_pre),
            low(d_gated * ssm_out * silu_slope(gate_pre)),
        )
        kept_gate.append(low_gate)
        d_state, back = None, []
        for pull, d_out in list(zip(scan_pulls, cut(d_ssm.reshape(sequence_length, heads, -1))))[::-1]:
            *found, d_state = yield pull((d_state, d_out))
            back.append(found)
        d_x, d_step, g_bias, g_decay, g_skip, d_in_map, d_out_map = zip(*back[::-1])
        d_value_act = jnp.concatenate(d_x, 0).reshape(sequence_length, -1)
        d_step = jnp.concatenate(d_step, 0)
        d_in_map, d_out_map = jnp.concatenate(d_in_map, 0), jnp.concatenate(d_out_map, 0)
        g_bias, g_decay, g_skip = sum(g_bias), sum(g_decay), sum(g_skip)
        map_keep = jnp.where(tensor_rank == 0, d_in_map, d_out_map)
        map_send = jnp.where(tensor_rank == 0, d_out_map, d_in_map)
        d_state_act = total_of(map_keep, grid.swap(low(map_send)))
        d_value, g_vkernel, g_voffset = value_pull(d_value_act)
        d_value, d_state_act = yield (low(d_value), d_state_act)
        d_state, g_skernel, g_soffset = state_pull(d_state_act)
        low_narrow = jnp.concatenate(
            [low(d_state), low(d_step), jnp.zeros((sequence_length, -narrow % 128), jnp.bfloat16)],
            1,
        )
        smalls = (g_ngated, g_vkernel, g_voffset, g_skernel, g_soffset, g_bias, g_decay, g_skip)
        return jnp.concatenate([d_value, low_narrow], 1), smalls

    mix_out_sum = sum_weight(after(low(times_over(dfull, mixed)), attention_sum))
    low_first, smalls = Beside(mixer_backward()).finish()
    (low_gate,) = kept_gate
    gate_sum = sum_weight(after(low(times_over(full, low_gate)), mix_out_sum))
    late_sums = grid.core_product(ordered, low_first)
    low_gate, low_first = after((low_gate, low_first), late_sums)
    d_normed = times_back(low_gate, w_gate) + times_back(low_first, w_first)
    d_normed = times_back(low(d_normed), order)
    d_rows, g_nmix = norm_pull(grid.pair_sum(d_normed, 0))
    grad = grad + d_rows
    g_ngated, g_vkernel, g_voffset, g_skernel, g_soffset, g_bias, g_decay, g_skip = smalls

    g_shared_one, g_experts_one = expert_grads(weights_one, low_first)
    shared_grads = jnp.concatenate([g_shared_one, g_shared_two], 1)
    shared_back = lax.all_to_all(
        shared_grads.reshape(expert_count, block_rows, 6 * shared_units),
        "dp",
        split_axis=0,
        concat_axis=0,
        tiled=True,
    ).astype(jnp.float32)
    shared_back = shared_back.reshape(expert_count, block_rows, 6, shared_units)
    shared_back = shared_back.transpose(2, 1, 0, 3).reshape(6, block_rows, -1)

    def spread(value, start, whole):
        value = value.reshape(-1, value.shape[-1])
        wide = jnp.zeros((value.shape[0], whole), jnp.float32)
        return lax.dynamic_update_slice_in_dim(wide, value, start, 1).reshape(-1)

    def pack_sums(pieces):
        packed = [piece.reshape(-1) for piece in pieces]
        packed.append(jnp.zeros((-sum(piece.size for piece in pieces) % 2048,), jnp.float32))
        return Beside(grid.all_sum(jnp.concatenate(packed).reshape(-1, 128)))

    def unpack_sums(work, pieces):
        packed, found, at = work.finish().reshape(-1), [], 0
        for piece in pieces:
            found.append(packed[at : at + piece.size])
            at += piece.size
        return found

    early = (g_router_one, g_router_two, g_nmoe_one, g_nattn, g_nmoe_two)
    late = (
        g_nmix,
        spread(g_ngated, value_start, DI),
        spread(g_vkernel, value_start, DI),
        spread(g_voffset, value_start, DI),
        spread(g_skernel, state_start, 2 * NS),
        spread(g_soffset, state_start, 2 * NS),
        spread(g_bias, head_start, MH),
        spread(g_decay, head_start, MH),
        spread(g_skip, head_start, MH),
    )
    early = unpack_sums(pack_sums(early), early)
    work = pack_sums(late)
    value_sum = grid.scatter_ordered(late_sums, work)
    late = unpack_sums(work, late)
    summed = early[:2] + late[:1] + early[2:] + late[1:]
    return (
        block_out,
        grad,
        gate_sum,
        value_sum[:, :value_cols],
        value_sum[:, value_cols : value_cols + state_cols],
        value_sum[:, value_cols + state_cols : value_cols + narrow],
        mix_out_sum.T,
        attention_sum[:, :q_cols],
        attention_sum[:, q_cols : q_cols + k_cols],
        attention_sum[:, q_cols + k_cols : wide_cols],
        attention_sum[:, wide_cols:].T,
        shared_back[0],
        shared_back[1],
        shared_back[2].T,
        shared_back[3],
        shared_back[4],
        shared_back[5].T,
        g_experts_one[0],
        g_experts_one[1],
        g_experts_one[2],
        g_experts_two[0],
        g_experts_two[1],
        g_experts_two[2],
        summed[0].reshape(expert_count, model).T,
        summed[1].reshape(expert_count, model).T,
        summed[2],
        summed[3],
        summed[4],
        summed[5],
        summed[6],
        summed[7].reshape(-1, DI),
        summed[8],
        summed[9].reshape(-1, 2 * NS),
        summed[10],
        summed[11],
        summed[12],
        summed[13],
    )


def solution(mesh):
    in_specs = (
        P(("dp", "tensor"), None),
        P(("dp", "tensor"), None),
        P("dp", None),
        P("dp", None),
        P("dp", "tensor"),
        P("dp", "tensor"),
        P("dp", "tensor"),
        P("dp", "tensor"),
        P("tensor", "dp"),
        P("dp", "tensor"),
        P("dp", "tensor"),
        P("dp", "tensor"),
        P("tensor", "dp"),
        P("dp", "tensor"),
        P("dp", "tensor"),
        P("tensor", "dp"),
        P("dp", "tensor"),
        P("dp", "tensor"),
        P("tensor", "dp"),
        P("dp", None, "tensor"),
        P("dp", None, "tensor"),
        P("dp", "tensor", None),
        P("dp", None, "tensor"),
        P("dp", None, "tensor"),
        P("dp", "tensor", None),
        P(),
        P(),
        P(),
        P(),
        P(),
        P(),
        P(),
        P(),
        P(),
        P(),
        P(),
        P(),
        P(),
        P(),
    )
    out_specs = (
        P(("dp", "tensor"), None),
        P(("dp", "tensor"), None),
        P("dp", "tensor"),
        P("dp", "tensor"),
        P("dp", "tensor"),
        P("dp", "tensor"),
        P("tensor", "dp"),
        P("dp", "tensor"),
        P("dp", "tensor"),
        P("dp", "tensor"),
        P("tensor", "dp"),
        P("dp", "tensor"),
        P("dp", "tensor"),
        P("tensor", "dp"),
        P("dp", "tensor"),
        P("dp", "tensor"),
        P("tensor", "dp"),
        P("dp", None, "tensor"),
        P("dp", None, "tensor"),
        P("dp", "tensor", None),
        P("dp", None, "tensor"),
        P("dp", None, "tensor"),
        P("dp", "tensor", None),
        P(),
        P(),
        P(),
        P(),
        P(),
        P(),
        P(),
        P(),
        P(),
        P(),
        P(),
        P(),
        P(),
        P(),
    )
    return jax.shard_map(body, mesh=mesh, in_specs=in_specs, out_specs=out_specs, check_vma=False)
```

time: 1310 us -> 1090 us (0.83)
  waiting for transfers between devices: 497 us -> 367 us
  starting transfers between devices: 231 us -> 171 us
  matrix products: 229 us -> 203 us
  blocking collectives: 20.6 us -> 0 us
    ppermute x229 -> x153, waiting for transfers between devices: 497 us -> 365 us  [shift(): return lax.ppermute(value, AXES, pairs)]
    ppermute x229 -> x153, starting transfers between devices: 220 us -> 164 us  [shift(): return lax.ppermute(value, AXES, pairs)]
    unnamed x803 -> x723, local copies, waits for them, and re-layouts: 60.3 us -> 100 us
    dot_general x25 -> x22, matrix products: 41.8 us -> 15.1 us  [the longest x6 9.01 us: scan_block(): jnp.einsum('ijh,jhp->ihp', weights, x_blk, precision=SCAN)]
    all_gather x1 -> x0, blocking collectives: 20.6 us -> none  [body(): lax.all_gather(low(jnp.concatenate([mask_one, mask_two], 1)), 'dp', axis=0)]
    concatenate x15 -> x33, other arithmetic: 5.73 us -> 24.4 us  [the longest x16 11.4 us: with_core(): half = jnp.concatenate(near, 0)]
    convert_element_type x79 -> x63, other arithmetic: 45.9 us -> 32.2 us  [low(): return value_rows.astype(jnp.bfloat16)]
    dot_general x24 -> x23, matrix products: 65.9 us -> 60.1 us  [times_back(): lax.dot_general(left, right, (((1,), (1,)), ((), ())), preferred_element_...]
  transfers between devices with their start and end apart: 232 -> 161, of which waited for: 103 -> 69; matrix products, arithmetic and copies ran while one was open for 32% -> 42% of each run, Pallas kernels for 0% -> 0%
where the time goes in v2:
time: 1090 us; the launch traced here: 1080 us
  waiting for transfers between devices  367 us (34%)
  matrix products  203 us (19%)
  local copies, waits for them, and re-layouts  188 us (17%)
  starting transfers between devices  171 us (16%)
  other arithmetic  130 us (12%)
  between operations  20.4 us (2%)
    ppermute x153, waiting for transfers between devices, shift(): return lax.ppermute(value, AXES, pairs)  365 us
    ppermute x153, starting transfers between devices, shift(): return lax.ppermute(value, AXES, pairs)  164 us
    unnamed x723, local copies, waits for them, and re-layouts  100 us
    dot_general x12, matrix products, times_over(): lax.dot_general(left, right, (((0,), (0,)), ((), ())), preferred_element_...  62.9 us
    dot_general x33, matrix products, matmul(): return jnp.dot(left, right, preferred_element_type=jnp.float32)  60.3 us
    dot_general x23, matrix products, times_back(): lax.dot_general(left, right, (((1,), (1,)), ((), ())), preferred_element_...  60.1 us
    convert_element_type x63, other arithmetic, low(): return value_rows.astype(jnp.bfloat16)  32.2 us
  transfers between devices with their start and end apart: 161, of which 69 were waited for; matrix products, arithmetic and copies ran while one was open for 42% of the time, Pallas kernels for 0%

profile of v2, /device:TPU:0, one launch (start us, length us, event | category | flops | bytes accessed | tf_op | source)
XLA Modules:
  0.0 1079.9 jit_solution(3918273480465605250)
XLA Ops:
  30.2 8.0 collective-permute-done.2
  41.1 12.4 %collective-permute-done.4 = bf16[96,1792]{1,0:T(8,128)(2,1)S(1)} collective-permute-done((bf16[96,1792]{1,0:T(8,128)(2,1)S(1)}, bf16[96,1792]{1,0:T(8,128)(2,1)S(1)}, u32[]{:S(2)}, u32[]{:S(2)}) %collective-permute-start.4) | collective-permute-done | bytes 344096 | tf_op jit(solution)/shard_map/ppermute | solution.py:159
  155.7 8.1 collective-permute-done.24
  186.0 9.9 collective-permute-done.25
  204.2 7.5 collective-permute-done.19
  216.9 7.3 collective-permute-done.20
  225.5 19.2 %collective-permute-done.28 = bf16[128,1536]{1,0:T(8,128)(2,1)S(1)} collective-permute-done((bf16[128,1536]{1,0:T(8,128)(2,1)S(1)}, bf16[128,1536]{1,0:T(8,128)(2,1)S(1)}, u32[]{:S(2)}, u32[]{:S(2)}) %collective-permute-start.28) | collective-permute-done | bytes 393248 | tf_op jit(solution)/shard_map/ppermute | solution.py:159
  261.6 12.1 %collective-permute-done.36 = bf16[128,1536]{1,0:T(8,128)(2,1)S(1)} collective-permute-done((bf16[128,1536]{1,0:T(8,128)(2,1)S(1)}, bf16[128,1536]{1,0:T(8,128)(2,1)S(1)}, u32[]{:S(2)}, u32[]{:S(2)}) %collective-permute-start.36) | collective-permute-done | bytes 393248 | tf_op jit(solution)/shard_map/ppermute | solution.py:159
  304.6 9.5 collective-permute-done.42
  316.1 9.0 collective-permute-done.43
  483.4 9.9 collective-permute-done.81
  495.6 9.0 collective-permute-done.82
  509.2 7.2 collective-permute-done.84
  532.7 14.7 %fusion.382 = (bf16[1536,1152]{0,1:T(8,128)(2,1)}, f32[1536,1152]{0,1:T(8,128)}) fusion(bf16[512,1536]{1,0:T(8,128)(2,1)} %copy-done.67, bf16[512,1536]{1,0:T(8,128)(2,1)S(1)} %copy-done.66, bf16[512,1536]{1,0:T(8,128)(2,1)S(1)} %constant_dynamic-update-slice_fusion.65, bf16[512,1536]{1,0:T(8,128)(2,1)} %copy-done.69, bf16[512,1152]{0,1:T(8,128)(2,1)} %copy-done.102, ...), kind=kOutput, calls=%fused_computation.976 | convolution fusion | flops 7293566976 | bytes 21626880 | tf_op jit(solution)/shard_map/dot_general | solution.py:32
  595.2 6.2 collective-permute-done.89
  616.2 7.5 collective-permute-done.91
  639.4 8.7 copy.719
  659.9 14.4 %collective-permute-done.105 = bf16[128,1536]{1,0:T(8,128)(2,1)S(1)} collective-permute-done((bf16[128,1536]{1,0:T(8,128)(2,1)}, bf16[128,1536]{1,0:T(8,128)(2,1)S(1)}, u32[]{:S(2)}, u32[]{:S(2)}) %collective-permute-start.105) | collective-permute-done | bytes 393248 | tf_op jit(solution)/shard_map/ppermute | solution.py:159
  686.5 9.6 collective-permute-done.109
  721.4 15.0 %collective-permute-done.112 = bf16[128,1664]{1,0:T(8,128)(2,1)S(1)} collective-permute-done((bf16[128,1664]{1,0:T(8,128)(2,1)S(1)}, bf16[128,1664]{1,0:T(8,128)(2,1)S(1)}, u32[]{:S(2)}, u32[]{:S(2)}) %collective-permute-start.112) | collective-permute-done | bytes 426016 | tf_op jit(solution)/shard_map/ppermute | solution.py:159
  737.9 10.9 %collective-permute-done.113 = bf16[128,1664]{1,0:T(8,128)(2,1)S(1)} collective-permute-done((bf16[128,1664]{1,0:T(8,128)(2,1)S(1)}, bf16[128,1664]{1,0:T(8,128)(2,1)S(1)}, u32[]{:S(2)}, u32[]{:S(2)}) %collective-permute-start.113) | collective-permute-done | bytes 426016 | tf_op jit(solution)/shard_map/ppermute | solution.py:159
  749.0 11.3 %collective-permute-done.114 = bf16[128,1664]{1,0:T(8,128)(2,1)S(1)} collective-permute-done((bf16[128,1664]{1,0:T(8,128)(2,1)S(1)}, bf16[128,1664]{1,0:T(8,128)(2,1)S(1)}, u32[]{:S(2)}, u32[]{:S(2)}) %collective-permute-start.114) | collective-permute-done | bytes 426016 | tf_op jit(solution)/shard_map/ppermute | solution.py:159
  763.9 7.1 collective-permute-done.115
  782.2 6.8 collective-permute-done.118
  896.6 7.8 fusion.3
  909.5 7.4 fusion.29
  918.8 14.6 %fusion.383 = (bf16[1536,1152]{0,1:T(8,128)(2,1)}, f32[1536,1152]{0,1:T(8,128)}) fusion(bf16[512,1536]{1,0:T(8,128)(2,1)S(1)} %copy-done.60, bf16[512,1536]{1,0:T(8,128)(2,1)S(1)} %copy-done.64, bf16[512,1536]{1,0:T(8,128)(2,1)S(1)} %copy-done.62, bf16[512,1536]{1,0:T(8,128)(2,1)} %copy-done.68, bf16[512,1152]{0,1:T(8,128)(2,1)} %copy-done.101, ...), kind=kOutput, calls=%fused_computation.977 | convolution fusion | flops 7293566976 | bytes 21626880 | tf_op jit(solution)/shard_map/dot_general | solution.py:32
  954.4 8.5 collective-permute-done.132
  986.4 13.1 %collective-permute-done.134 = bf16[96,1792]{1,0:T(8,128)(2,1)S(1)} collective-permute-done((bf16[96,1792]{1,0:T(8,128)(2,1)S(1)}, bf16[96,1792]{1,0:T(8,128)(2,1)S(1)}, u32[]{:S(2)}, u32[]{:S(2)}) %collective-permute-start.134) | collective-permute-done | bytes 344096 | tf_op jit(solution)/shard_map/ppermute | solution.py:159
  999.4 10.5 collective-permute-start.138
  1023.2 8.8 collective-permute-done.137
  1055.1 11.0 %collective-permute-done.144 = bf16[256,1536]{1,0:T(8,128)(2,1)} collective-permute-done((bf16[256,1536]{1,0:T(8,128)(2,1)}, bf16[256,1536]{1,0:T(8,128)(2,1)}, u32[]{:S(2)}, u32[]{:S(2)}) %collective-permute-start.144) | collective-permute-done | bytes 786464 | tf_op jit(solution)/shard_map/ppermute | solution.py:159
  (1521 shorter events, 736.4 us)
Async XLA Ops:
  7.3 159.3 %all-gather.9.cloned.1.call-start = ((), (), s32[]{:S(2)}) async-start(), calls=%async_computation.9 | async-start | bytes 1671168 | tf_op jit(solution)/shard_map/all_gather | solution.py:477
  10.0 186.6 %all-gather.5.cloned.1.call-start = ((), (), s32[]{:S(2)}) async-start(), calls=%async_computation.5 | async-start | bytes 5013504 | tf_op jit(solution)/shard_map/all_gather | solution.py:409
  19.8 68.2 %collective-permute-start.10 = (bf16[128,1536]{1,0:T(8,128)(2,1)}, bf16[128,1536]{1,0:T(8,128)(2,1)}, u32[]{:S(2)}, u32[]{:S(2)}) collective-permute-start(bf16[128,1536]{1,0:T(8,128)(2,1)} %fusion.185), channel_id=1, source_target_pairs={{0,1},{1,0},{2,3},{3,2},{4,5},{5,4},{6,7},{7,6},{8,9},{9,8},{10,11... | collective-permute-start | bytes 1179656 | tf_op jit(solution)/shard_map/ppermute | solution.py:159
  64.7 28.1 %collective-permute-start.7 = (bf16[768,1792]{1,0:T(8,128)(2,1)}, bf16[768,1792]{1,0:T(8,128)(2,1)S(1)}, u32[]{:S(2)}, u32[]{:S(2)}) collective-permute-start(bf16[768,1792]{1,0:T(8,128)(2,1)} %get-tuple-element.925), channel_id=1, source_target_pairs={{0,2},{1,3},{2,0},{3,1},{4,6},{5,7},{6,4},{7,5},{8,10},{9,11},{10,... | collective-permute-start | bytes 8257544 | tf_op jit(solution)/shard_map/ppermute | solution.py:159
  89.6 54.2 %collective-permute-start.23 = (bf16[1536,256]{1,0:T(8,128)(2,1)}, bf16[1536,256]{1,0:T(8,128)(2,1)}, u32[]{:S(2)}, u32[]{:S(2)}) collective-permute-start(bf16[1536,256]{1,0:T(8,128)(2,1)} %bitcast.16), channel_id=1, source_target_pairs={{0,1},{1,0},{2,3},{3,2},{4,5},{5,4},{6,7},{7,6},{8,9},{9,8},{10,11... | collective-permute-start | bytes 2359304 | tf_op jit(solution)/shard_map/ppermute | solution.py:159
  142.9 32.8 %collective-permute-start.17 = (bf16[768,1536]{1,0:T(8,128)(2,1)}, bf16[768,1536]{1,0:T(8,128)(2,1)}, u32[]{:S(2)}, u32[]{:S(2)}) collective-permute-start(bf16[768,1536]{1,0:T(8,128)(2,1)} %get-tuple-element.941), channel_id=1, source_target_pairs={{0,2},{1,3},{2,0},{3,1},{4,6},{5,7},{6,4},{7,5},{8,10},{9,11},{10,... | collective-permute-start | bytes 7077896 | tf_op jit(solution)/shard_map/ppermute | solution.py:159
  154.7 205.9 %all-gather.7.cloned.1.call-start = ((), (), s32[]{:S(2)}) async-start(), calls=%async_computation.6 | async-start | bytes 6684672 | tf_op jit(solution)/shard_map/all_gather | solution.py:410
  163.9 121.0 %collective-permute-start.26 = (bf16[256,1536]{1,0:T(8,128)(2,1)}, bf16[256,1536]{1,0:T(8,128)(2,1)}, u32[]{:S(2)}, u32[]{:S(2)}) collective-permute-start(bf16[256,1536]{1,0:T(8,128)(2,1)} %bitcast.18), channel_id=1, source_target_pairs={{0,1},{1,0},{2,3},{3,2},{4,5},{5,4},{6,7},{7,6},{8,9},{9,8},{10,11... | collective-permute-start | bytes 2359304 | tf_op jit(solution)/shard_map/ppermute | solution.py:159
  214.6 30.7 %collective-permute-start.39 = (bf16[1536,256]{1,0:T(8,128)(2,1)}, bf16[1536,256]{1,0:T(8,128)(2,1)}, u32[]{:S(2)}, u32[]{:S(2)}) collective-permute-start(bf16[1536,256]{1,0:T(8,128)(2,1)} %bitcast.46), channel_id=1, source_target_pairs={{0,1},{1,0},{2,3},{3,2},{4,5},{5,4},{6,7},{7,6},{8,9},{9,8},{10,11... | collective-permute-start | bytes 2359304 | tf_op jit(solution)/shard_map/ppermute | solution.py:159
  216.8 746.1 %reduce-scatter.10.cloned.1.call-start = ((), (), s32[]{:S(2)}) async-start(), calls=%async_computation.10 | async-start | bytes 6684672
  225.4 31.1 %collective-permute-start.22 = (bf16[256,1536]{1,0:T(8,128)(2,1)S(1)}, bf16[256,1536]{1,0:T(8,128)(2,1)S(1)}, u32[]{:S(2)}, u32[]{:S(2)}) collective-permute-start(bf16[256,1536]{1,0:T(8,128)(2,1)S(1)} %pad_maximum_fusion.21), channel_id=1, source_target_pairs={{0,2},{1,3},{2,0},{3,1},{4,6},{5,7},{6,4},{7,5},{8,10},{9,11},{10,... | collective-permute-start | bytes 2359304 | tf_op jit(solution)/shard_map/ppermute | solution.py:159
  260.6 39.4 %collective-permute-start.41 = (bf16[256,1536]{1,0:T(8,128)(2,1)S(1)}, bf16[256,1536]{1,0:T(8,128)(2,1)S(1)}, u32[]{:S(2)}, u32[]{:S(2)}) collective-permute-start(bf16[256,1536]{1,0:T(8,128)(2,1)S(1)} %bitcast.437), channel_id=1, source_target_pairs={{0,1},{1,0},{2,3},{3,2},{4,5},{5,4},{6,7},{7,6},{8,9},{9,8},{10,11... | collective-permute-start | bytes 2359304 | tf_op jit(solution)/shard_map/ppermute | solution.py:159
  376.5 35.9 %collective-permute-start.70 = (bf16[256,1536]{1,0:T(8,128)(2,1)}, bf16[256,1536]{1,0:T(8,128)(2,1)}, u32[]{:S(2)}, u32[]{:S(2)}) collective-permute-start(bf16[256,1536]{1,0:T(8,128)(2,1)} %pad_maximum_fusion.29), channel_id=1, source_target_pairs={{0,2},{1,3},{2,0},{3,1},{4,6},{5,7},{6,4},{7,5},{8,10},{9,11},{10,... | collective-permute-start | bytes 2359304 | tf_op jit(solution)/shard_map/ppermute | solution.py:159
  399.1 27.8 %collective-permute-start.72 = (bf16[256,1536]{1,0:T(8,128)(2,1)S(1)}, bf16[256,1536]{1,0:T(8,128)(2,1)S(1)}, u32[]{:S(2)}, u32[]{:S(2)}) collective-permute-start(bf16[256,1536]{1,0:T(8,128)(2,1)S(1)} %pad_maximum_fusion.30), channel_id=1, source_target_pairs={{0,2},{1,3},{2,0},{3,1},{4,6},{5,7},{6,4},{7,5},{8,10},{9,11},{10,... | collective-permute-start | bytes 2359304 | tf_op jit(solution)/shard_map/ppermute | solution.py:159
  477.9 28.9 %collective-permute-start.71 = (bf16[256,1664]{1,0:T(8,128)(2,1)S(1)}, bf16[256,1664]{1,0:T(8,128)(2,1)S(1)}, u32[]{:S(2)}, u32[]{:S(2)}) collective-permute-start(bf16[256,1664]{1,0:T(8,128)(2,1)S(1)} %pad_maximum_fusion.20), channel_id=1, source_target_pairs={{0,2},{1,3},{2,0},{3,1},{4,6},{5,7},{6,4},{7,5},{8,10},{9,11},{10,... | collective-permute-start | bytes 2555912 | tf_op jit(solution)/shard_map/ppermute | solution.py:159
  479.7 38.9 %collective-permute-start.58 = (bf16[256,1536]{1,0:T(8,128)(2,1)S(1)}, bf16[256,1536]{1,0:T(8,128)(2,1)S(1)}, u32[]{:S(2)}, u32[]{:S(2)}) collective-permute-start(bf16[256,1536]{1,0:T(8,128)(2,1)S(1)} %slice.935), channel_id=1, source_target_pairs={{0,2},{1,3},{2,0},{3,1},{4,6},{5,7},{6,4},{7,5},{8,10},{9,11},{10,... | collective-permute-start | bytes 2359304 | tf_op jit(solution)/shard_map/ppermute | solution.py:159
  572.1 42.0 %collective-permute-start.121 = (bf16[1536,256]{0,1:T(8,128)(2,1)}, bf16[1536,256]{0,1:T(8,128)(2,1)}, u32[]{:S(2)}, u32[]{:S(2)}) collective-permute-start(bf16[1536,256]{0,1:T(8,128)(2,1)} %get-tuple-element.425), channel_id=1, source_target_pairs={{0,1},{1,0},{2,3},{3,2},{4,5},{5,4},{6,7},{7,6},{8,9},{9,8},{10,11... | collective-permute-start | bytes 2359304 | tf_op jit(solution)/shard_map/ppermute | solution.py:159
  614.1 38.2 %collective-permute-start.122 = (bf16[1536,256]{0,1:T(8,128)(2,1)}, bf16[1536,256]{0,1:T(8,128)(2,1)}, u32[]{:S(2)}, u32[]{:S(2)}) collective-permute-start(bf16[1536,256]{0,1:T(8,128)(2,1)} %get-tuple-element.426), channel_id=1, source_target_pairs={{0,1},{1,0},{2,3},{3,2},{4,5},{5,4},{6,7},{7,6},{8,9},{9,8},{10,11... | collective-permute-start | bytes 2359304 | tf_op jit(solution)/shard_map/ppermute | solution.py:159
  639.2 37.8 %collective-permute-start.99 = (bf16[256,1536]{1,0:T(8,128)(2,1)}, bf16[256,1536]{1,0:T(8,128)(2,1)}, u32[]{:S(2)}, u32[]{:S(2)}) collective-permute-start(bf16[256,1536]{1,0:T(8,128)(2,1)} %pad_maximum_fusion.33), channel_id=1, source_target_pairs={{0,2},{1,3},{2,0},{3,1},{4,6},{5,7},{6,4},{7,5},{8,10},{9,11},{10,... | collective-permute-start | bytes 2359304 | tf_op jit(solution)/shard_map/ppermute | solution.py:159
  648.2 420.9 %reduce-scatter.8.cloned.1.call-start = ((), (), s32[]{:S(2)}) async-start(), calls=%async_computation.8 | async-start | bytes 5013504 | tf_op jit(solution)/shard_map/reduce_scatter | solution.py:590
  650.9 155.6 %collective-permute-start.95 = (bf16[128,1536]{1,0:T(8,128)(2,1)}, bf16[128,1536]{1,0:T(8,128)(2,1)}, u32[]{:S(2)}, u32[]{:S(2)}) collective-permute-start(bf16[128,1536]{1,0:T(8,128)(2,1)} %slice.790), channel_id=1, source_target_pairs={{0,4},{1,5},{2,6},{3,7},{4,0},{5,1},{6,2},{7,3},{8,12},{9,13},{10,... | collective-permute-start | bytes 1179656 | tf_op jit(solution)/shard_map/ppermute | solution.py:159
  652.3 156.2 %collective-permute-start.96 = (bf16[128,1536]{1,0:T(8,128)(2,1)}, bf16[128,1536]{1,0:T(8,128)(2,1)}, u32[]{:S(2)}, u32[]{:S(2)}) collective-permute-start(bf16[128,1536]{1,0:T(8,128)(2,1)} %add_convert_fusion.21), channel_id=1, source_target_pairs={{0,24},{1,25},{2,26},{3,27},{4,28},{5,29},{6,30},{7,31},{8,0},{9,1... | collective-permute-start | bytes 1179656 | tf_op jit(solution)/shard_map/ppermute | solution.py:159
  674.3 118.8 %collective-permute-start.123 = (bf16[256,1536]{1,0:T(8,128)(2,1)}, bf16[256,1536]{1,0:T(8,128)(2,1)}, u32[]{:S(2)}, u32[]{:S(2)}) collective-permute-start(bf16[256,1536]{1,0:T(8,128)(2,1)} %slice.1400), channel_id=1, source_target_pairs={{0,1},{1,0},{2,3},{3,2},{4,5},{5,4},{6,7},{7,6},{8,9},{9,8},{10,11... | collective-permute-start | bytes 2359304 | tf_op jit(solution)/shard_map/ppermute | solution.py:159
  736.4 25.2 %collective-permute-start.100 = (bf16[256,1664]{1,0:T(8,128)(2,1)S(1)}, bf16[256,1664]{1,0:T(8,128)(2,1)S(1)}, u32[]{:S(2)}, u32[]{:S(2)}) collective-permute-start(bf16[256,1664]{1,0:T(8,128)(2,1)S(1)} %pad_maximum_fusion.16), channel_id=1, source_target_pairs={{0,2},{1,3},{2,0},{3,1},{4,6},{5,7},{6,4},{7,5},{8,10},{9,11},{10,... | collective-permute-start | bytes 2555912 | tf_op jit(solution)/shard_map/ppermute | solution.py:159
  808.5 53.1 %collective-permute-start.147 = (f32[216,128]{1,0:T(8,128)S(1)}, f32[216,128]{1,0:T(8,128)}, u32[]{:S(2)}, u32[]{:S(2)}) collective-permute-start(f32[216,128]{1,0:T(8,128)S(1)} %add.1131), channel_id=1, source_target_pairs={{0,4},{1,5},{2,6},{3,7},{4,0},{5,1},{6,2},{7,3},{8,12},{9,13},{10,... | collective-permute-start | bytes 331784 | tf_op jit(solution)/shard_map/ppermute | solution.py:159
  859.6 28.0 %collective-permute-start.126 = (bf16[768,1792]{1,0:T(8,128)(2,1)}, bf16[768,1792]{1,0:T(8,128)(2,1)}, u32[]{:S(2)}, u32[]{:S(2)}) collective-permute-start(bf16[768,1792]{1,0:T(8,128)(2,1)} %convolution_convert_fusion.4), channel_id=1, source_target_pairs={{0,2},{1,3},{2,0},{3,1},{4,6},{5,7},{6,4},{7,5},{8,10},{9,11},{10,... | collective-permute-start | bytes 8257544 | tf_op jit(solution)/shard_map/ppermute | solution.py:159
  882.3 188.6 %reduce-scatter.6.cloned.1.call-start = ((), (), s32[]{:S(2)}) async-start(), calls=%async_computation.7 | async-start | bytes 5013504 | tf_op jit(solution)/shard_map/reduce_scatter | solution.py:590
  907.1 37.8 %collective-permute-start.127 = (bf16[128,1536]{1,0:T(8,128)(2,1)}, bf16[128,1536]{1,0:T(8,128)(2,1)}, u32[]{:S(2)}, u32[]{:S(2)}) collective-permute-start(bf16[128,1536]{1,0:T(8,128)(2,1)} %dynamic-slice_convert_fusion), channel_id=1, source_target_pairs={{0,1},{1,0},{2,3},{3,2},{4,5},{5,4},{6,7},{7,6},{8,9},{9,8},{10,11... | collective-permute-start | bytes 1179656 | tf_op jit(solution)/shard_map/ppermute | solution.py:159
  907.6 39.6 %collective-permute-start.128 = (bf16[96,1792]{1,0:T(8,128)(2,1)}, bf16[96,1792]{1,0:T(8,128)(2,1)}, u32[]{:S(2)}, u32[]{:S(2)}) collective-permute-start(bf16[96,1792]{1,0:T(8,128)(2,1)} %slice.1003), channel_id=1, source_target_pairs={{0,4},{1,5},{2,6},{3,7},{4,0},{5,1},{6,2},{7,3},{8,12},{9,13},{10,... | collective-permute-start | bytes 1032200 | tf_op jit(solution)/shard_map/ppermute | solution.py:159
  942.9 75.6 %collective-permute-start.142 = (bf16[1536,256]{0,1:T(8,128)(2,1)}, bf16[1536,256]{0,1:T(8,128)(2,1)}, u32[]{:S(2)}, u32[]{:S(2)}) collective-permute-start(bf16[1536,256]{0,1:T(8,128)(2,1)} %get-tuple-element.466), channel_id=1, source_target_pairs={{0,1},{1,0},{2,3},{3,2},{4,5},{5,4},{6,7},{7,6},{8,9},{9,8},{10,11... | collective-permute-start | bytes 2359304 | tf_op jit(solution)/shard_map/ppermute | solution.py:159
  972.8 61.5 %all-to-all-start.1 = ((bf16[16,96,192]{1,2,0:T(8,128)(2,1)}), bf16[16,96,192]{1,2,0:T(8,128)(2,1)S(1)}, u32[]{:S(2)}, u32[]{:S(2)}) async-start(bf16[16,96,192]{1,2,0:T(8,128)(2,1)} %copy.675), calls=%async_computation.3 | async-start | bytes 1572864 | tf_op jit(solution)/shard_map/all_to_all | solution.py:778
  1018.5 27.4 %collective-permute-start.143 = (bf16[1536,256]{0,1:T(8,128)(2,1)S(1)}, bf16[1536,256]{0,1:T(8,128)(2,1)}, u32[]{:S(2)}, u32[]{:S(2)}) collective-permute-start(bf16[1536,256]{0,1:T(8,128)(2,1)S(1)} %copy-done.127), channel_id=1, source_target_pairs={{0,1},{1,0},{2,3},{3,2},{4,5},{5,4},{6,7},{7,6},{8,9},{9,8},{10,11... | collective-permute-start | bytes 2359304 | tf_op jit(solution)/shard_map/ppermute | solution.py:159
  (438 other events, 4029.1 us)
Sparse Core Ops, SparseCore 0:
  10.8 48.1 all-gather.8
  61.3 63.8 all-gather.4
  216.9 76.8 all-gather.6
  648.3 95.6 reduce-scatter.9
  882.4 83.1 reduce-scatter.7
  969.3 86.9 reduce-scatter.5
